TPU v7x, 128 devices: a whole 4x4x4 slice. The times are simulated.
128 devices in a mesh: tm: 2 (over z_hi), clip: 64 (over z_lo, x, y, core).
Axes of the slice: x: 4, y: 4, z: 4 (z_hi: 2, z_lo: 2; z = z_hi * 2 + z_lo), core: 2. Of those that a mesh axis runs over, the one named last changes fastest.
Arguments:
- frames: bfloat16 [16384, 16, 1408], P('clip', 'tm'), may hold values from -32 to 32
- key_proj: bfloat16 [1408, 16], replicated, may hold values from -2 to 2
- value_weight: bfloat16 [1408, 1408], replicated, may hold values from -0.15625 to 0.15625
- out_weight: bfloat16 [1408, 512], replicated, may hold values from -0.15625 to 0.15625
- texts: bfloat16 [16384, 512], P(('tm', 'clip')), may hold values from -6 to 6
- logit_scale: float32 [1], replicated, may hold values from 4 to 12
- logit_bias: float32 [1], replicated, may hold values from -8 to -4
Outputs:
- grad_frames: bfloat16 [16384, 16, 1408], P('clip', 'tm')
- grad_texts: float32 [16384, 512], P(('tm', 'clip'))
All inputs are finite; a program needn't handle non-finite values.
Results may differ from a plain program's by a relative error of at most 0.02.
Values may be sent and summed in bfloat16 or wider, within the bound.
A program may use at most 192 MiB of HBM per device.

v0:
```python
import math

import jax
import jax.numpy as jnp
from jax import lax
from jax.sharding import PartitionSpec as P

EPSILON = 1e-06


def repeat_heads(per_head, head_size):
    return jnp.repeat(per_head, head_size, axis=1)


def weighted_values(exponent, values, head_count):
    clip_count, frame_count, model_width = values.shape
    head_size = model_width // head_count
    split_values = values.reshape(clip_count, frame_count, head_count, head_size)
    summed = jnp.einsum("cfh,cfhk->chk", exponent, split_values, preferred_element_type=jnp.float32)
    return summed.reshape(clip_count, model_width)


def pair_terms(vis_rows, text_rows, clip_ids, text_ids, logit_scale, logit_bias, inverse):
    logits = (
        lax.dot_general(
            vis_rows, text_rows, (((1,), (1,)), ((), ())), preferred_element_type=jnp.float32
        )
        * logit_scale[0]
        + logit_bias[0]
    )
    target_sign = jnp.where(clip_ids[:, None] == text_ids[None, :], 1.0, -1.0)
    return (
        logit_scale[0] * (-inverse * target_sign * jax.nn.sigmoid(-target_sign * logits))
    ).astype(jnp.bfloat16)


def local(frames, key_proj, value_weight, out_weight, texts, logit_scale, logit_bias):
    clip_count, frame_count, model_width = frames.shape
    head_count = key_proj.shape[1]
    head_size = model_width // head_count
    frame_rows = frames.reshape(clip_count * frame_count, model_width)
    scores = jnp.dot(frame_rows, key_proj, preferred_element_type=jnp.float32).reshape(
        clip_count, frame_count, head_count
    ) * (1.0 / math.sqrt(model_width))
    values = (
        jnp.dot(frame_rows, value_weight, preferred_element_type=jnp.float32)
        .astype(jnp.bfloat16)
        .reshape(clip_count, frame_count, model_width)
    )
    local_max = jnp.max(scores, axis=1)
    global_max = lax.pmax(local_max, "tm")
    exponent = jnp.exp(scores - global_max[:, None, :])
    global_sum, weighted = lax.psum(
        (jnp.sum(exponent, axis=1), weighted_values(exponent, values, head_count)), "tm"
    )
    pooled_sum = weighted / repeat_heads(global_sum, head_size)
    pooled = pooled_sum.astype(jnp.bfloat16)
    embedding = jnp.dot(pooled, out_weight, preferred_element_type=jnp.float32)
    vis_norm = jnp.sqrt(jnp.sum(embedding * embedding, axis=1, keepdims=True) + EPSILON)
    vis_unit = embedding / vis_norm
    vis_half = vis_unit.astype(jnp.bfloat16)
    text_full = texts.astype(jnp.float32)
    text_norm = jnp.sqrt(jnp.sum(text_full * text_full, axis=1, keepdims=True) + EPSILON)
    text_unit = text_full / text_norm
    text_half = text_unit.astype(jnp.bfloat16)
    clip_size = lax.axis_size("clip")
    clip_index = lax.axis_index("clip")
    all_clips = clip_count * clip_size
    inverse = 1.0 / all_clips
    gathered = lax.all_gather(text_half, "clip", axis=0, tiled=True)
    clip_ids = clip_index * clip_count + jnp.arange(clip_count, dtype=jnp.int32)
    text_ids = lax.axis_index("tm") * gathered.shape[0] + jnp.arange(
        gathered.shape[0], dtype=jnp.int32
    )
    logit_grad = pair_terms(
        vis_half, gathered, clip_ids, text_ids, logit_scale, logit_bias, inverse
    )
    vis_part = jnp.dot(logit_grad, gathered, preferred_element_type=jnp.float32)
    text_terms = lax.dot_general(
        logit_grad, vis_half, (((0,), (0,)), ((), ())), preferred_element_type=jnp.float32
    )
    text_grad = lax.psum_scatter(text_terms, "clip", scatter_dimension=0, tiled=True)
    vis_grad = lax.psum(vis_part.astype(jnp.bfloat16), "tm").astype(jnp.float32)
    grad_texts = (
        text_grad - text_unit * jnp.sum(text_grad * text_unit, axis=1, keepdims=True)
    ) / text_norm
    emb_grad = (
        (vis_grad - vis_unit * jnp.sum(vis_grad * vis_unit, axis=1, keepdims=True)) / vis_norm
    ).astype(jnp.bfloat16)
    pooled_grad = lax.dot_general(
        emb_grad, out_weight, (((1,), (1,)), ((), ())), preferred_element_type=jnp.float32
    )
    weights = jnp.exp(scores - global_max[:, None, :]) / global_sum[:, None, :]
    weight_wide = jnp.repeat(weights, head_size, axis=2)
    value_grad = (
        (weight_wide * pooled_grad[:, None, :])
        .astype(jnp.bfloat16)
        .reshape(clip_count * frame_count, model_width)
    )
    spread = pooled_grad[:, None, :] * (values.astype(jnp.float32) - pooled_sum[:, None, :])
    inner_sum = jnp.sum(spread.reshape(clip_count, frame_count, head_count, head_size), axis=3)
    score_grad = (
        (weights * inner_sum * (1.0 / math.sqrt(model_width)))
        .astype(jnp.bfloat16)
        .reshape(clip_count * frame_count, head_count)
    )
    total = lax.dot_general(
        value_grad, value_weight, (((1,), (1,)), ((), ())), preferred_element_type=jnp.float32
    )
    total = total + lax.dot_general(
        score_grad, key_proj, (((1,), (1,)), ((), ())), preferred_element_type=jnp.float32
    )
    grad_frames = total.astype(jnp.bfloat16).reshape(clip_count, frame_count, model_width)
    return (grad_frames, grad_texts)


def solution(mesh):
    in_specs = (P("clip", "tm", None), P(), P(), P(), P(("tm", "clip"), None), P(), P())
    out_specs = (P("clip", "tm", None), P(("tm", "clip"), None))
    return jax.shard_map(local, mesh=mesh, in_specs=in_specs, out_specs=out_specs, check_vma=False)
```

profile of v0, /device:TPU:0, one launch (start us, length us, event | category | flops | bytes accessed | tf_op | source)
XLA Modules:
  0.0 564.0 jit_solution(10540455673871579644)
XLA Ops:
  8.0 0.0 copy-start
  8.0 0.0 all-reduce.3.cloned.1.call-start
  8.1 4.5 fusion.37
  12.6 13.8 %pmax.7 = f32[256,16]{1,0:T(8,128)S(1)} all-reduce(f32[256,16]{1,0:T(8,128)S(1)} %get-tuple-element.4), channel_id=1, replica_groups=mesh['tm'=2,'clip'=64] {'tm'}, use_global_device_ids=true, to_apply=%region_1.0 | all-reduce | flops 4096 | bytes 32768 | tf_op jit(solution)/shard_map/pmax | solution.py:51
  26.4 0.4 fusion.17
  26.9 9.6 %psum.21 = f32[256,16]{1,0:T(8,128)S(1)} all-reduce(f32[256,16]{1,0:T(8,128)S(1)} %fusion.17), channel_id=1, replica_groups=mesh['tm'=2,'clip'=64] {'tm'}, use_global_device_ids=true, to_apply=%region_3.0 | all-reduce | flops 4096 | bytes 32768 | tf_op jit(solution)/shard_map/psum | solution.py:53
  36.5 0.0 copy-start.7
  36.5 1.6 fusion.15
  38.1 14.5 %convolution_convert_fusion = bf16[2048,1408]{1,0:T(8,128)(2,1)} fusion(bf16[1408,1408]{1,0:T(8,128)(2,1)} %param.9, bf16[256,8,1408]{2,1,0:T(8,128)(2,1)} %param.7), kind=kOutput, calls=%fused_computation.17 | convolution fusion | flops 8123056128 | bytes 15499264 | tf_op jit(solution)/shard_map/dot_general | solution.py:46
  52.6 0.0 copy-done.7
  52.6 18.8 %reshape_reshape.3 = bf16[256,8,16,88]{3,2,1,0:T(8,128)(2,1)} reshape(bf16[2048,1408]{1,0:T(8,128)(2,1)} %convolution_convert_fusion) | data formatting | bytes 11534336 | tf_op jit(solution)/shard_map/reshape;reshape | solution.py:18
  71.4 6.6 %multiply_reduce_fusion = f32[256,16,88]{2,1,0:T(8,128)S(1)} fusion(f32[256,16,8]{1,2,0:T(8,128)} %get-tuple-element.2, bf16[256,8,16,88]{3,2,1,0:T(8,128)(2,1)} %reshape_reshape.3), kind=kLoop, calls=%fused_computation | loop fusion | flops 8290304 | bytes 7340032
  78.0 1.7 copy.29
  79.7 0.0 all-reduce.3.cloned.1.call-update
  79.7 0.0 all-gather.2.cloned.1.call-start
  79.8 1.0 fusion.26
  80.8 1.7 fusion.36
  82.5 0.0 all-gather.2.cloned.1.call-update
  82.5 0.2 all-reduce.5.cloned.1.call-start
  82.7 1.0 copy.18
  85.1 54.5 %all-reduce.3.cloned.1.call-done = f32[256,1408]{0,1:T(8,128)} async-done(((f32[256,1408]{0,1:T(8,128)}), f32[256,1408]{0,1:T(8,128)}) %all-reduce.3.cloned.1.call-update) | async-done | bytes 1441808 | tf_op jit(solution)/shard_map/psum | solution.py:53
  139.6 1.5 bitcast_divide_fusion
  141.1 0.0 copy-done
  141.1 0.7 multiply_reduce_fusion.2
  141.8 0.0 copy-start.3
  141.8 76.3 %all-gather.2.cloned.1.call-done = bf16[8192,512]{1,0:T(8,128)(2,1)} async-done(((bf16[128,512]{1,0:T(8,128)(2,1)}), bf16[8192,512]{1,0:T(8,128)(2,1)}) %all-gather.2.cloned.1.call-update) | async-done | bytes 8388624 | tf_op jit(solution)/shard_map/all_gather | solution.py:70
  218.1 0.0 copy-start.9
  218.1 7.7 %fusion.9 = bf16[256,8192]{1,0:T(8,128)(2,1)S(1)} fusion(bf16[8192,512]{1,0:T(8,128)(2,1)} %all-gather.2.cloned.1.call-done, f32[]{:T(128)} %bitcast.42, s32[8192]{0:T(1024)S(1)} %iota_add_fusion, f32[]{:T(128)} %bitcast.41, s32[256]{0:T(256)S(1)} %iota_add_fusion.1, f32[256,512]{1,0:T(8,128)S(1)} %get-tuple-element.7, f32[256]{0:T(256)S(1)} %add_sqrt_fusion), kind=kOutput, calls=%fused_computation.16 | convolution fusion | flops 2175008768 | bytes 13142024 | tf_op jit(solution)/shard_map/dot_general | solution.py:25
  225.7 0.0 copy-start.4
  225.7 2.0 copy-done.4
  227.7 0.0 copy-done.9
  227.7 3.0 convolution_convert_fusion.1
  230.8 0.0 all-reduce.5.cloned.1.call-update
  230.8 0.0 reduce-scatter.2.cloned.1.call-start
  230.8 10.3 %fusion.31 = f32[8192,512]{1,0:T(8,128)} fusion(bf16[256,8192]{1,0:T(8,128)(2,1)} %copy-done.4, f32[256,512]{1,0:T(8,128)S(1)} %get-tuple-element.7, f32[256]{0:T(256)S(1)} %add_sqrt_fusion), kind=kOutput, calls=%fused_computation.49 | convolution fusion | flops 2147745792 | bytes 21496832 | tf_op jit(solution)/shard_map/dot_general | solution.py:79
  241.2 0.0 reduce-scatter.2.cloned.1.call-update
  241.2 9.8 %broadcast_in_dim.12 = f32[256,8,16,88]{3,2,1,0:T(8,128)} broadcast(f32[256,8,16]{2,1,0:T(8,128)} %get-tuple-element.3), dimensions={0,1,2} | broadcast | bytes 11665408 | tf_op jit(solution)/shard_map/broadcast_in_dim | solution.py:94
  251.0 17.4 %reshape.60 = f32[2048,1408]{1,0:T(8,128)} reshape(f32[256,8,16,88]{3,2,1,0:T(8,128)} %broadcast_in_dim.12) | data formatting | bytes 23068672 | tf_op jit(solution)/shard_map/reshape | solution.py:94
  268.4 1.9 copy.21
  270.3 0.0 all-reduce.5.cloned.1.call-done
  270.3 0.0 copy-done.3
  270.3 1.2 fusion.20
  271.5 0.0 copy-start.2
  271.5 3.0 fusion.27
  274.5 2.9 copy.19
  277.4 3.0 copy.20
  280.4 0.0 copy-done.2
  280.4 0.0 copy-start.6
  280.4 0.0 copy-start.10
  280.4 7.2 %multiply_reduce_fusion.1 = f32[256,8,16]{2,1,0:T(8,128)S(1)} fusion(bf16[256,8,16,88]{3,2,1,0:T(8,128)(2,1)} %reshape_reshape.3, f32[256,16,88]{2,1,0:T(8,128)S(1)} %copy-done.2, f32[256,16,88]{2,1,0:T(8,128)} %copy.20), kind=kLoop, calls=%fused_computation.1 | loop fusion | flops 11501568 | bytes 8781824 | tf_op jit(solution)/shard_map/reduce_sum | solution.py:101
  287.7 0.0 copy-done.6
  287.7 0.0 copy-done.10
  287.7 0.0 copy-start.1
  287.7 0.0 copy-start.8
  287.7 15.5 %fusion.10 = f32[2048,1408]{1,0:T(8,128)} fusion(bf16[1408,1408]{1,0:T(8,128)(2,1)S(1)} %copy-done.10, f32[2048,1408]{1,0:T(8,128)} %reshape.60, f32[256,1408]{1,0:T(8,128)S(1)} %copy-done.6), kind=kOutput, calls=%fused_computation.18 | convolution fusion | flops 8125939712 | bytes 28475392 | tf_op jit(solution)/shard_map/dot_general | solution.py:107
  303.2 0.0 copy-done.1
  303.2 0.0 copy-done.8
  303.2 0.0 copy-start.5
  303.2 8.6 %fusion.14 = bf16[256,8,1408]{2,1,0:T(8,128)(2,1)} fusion(f32[2048,1408]{1,0:T(8,128)} %fusion.10, bf16[1408,16]{0,1:T(8,128)(2,1)S(1)} %copy-done.8, f32[256,8,16]{2,1,0:T(8,128)S(1)} %copy-done.1, f32[256,8,16]{2,1,0:T(8,128)S(1)} %multiply_reduce_fusion.1), kind=kOutput, calls=%fused_computation.21 | convolution fusion | flops 98140160 | bytes 17608704 | tf_op jit(solution)/shard_map/dot_general | solution.py:110
  311.9 241.8 %reduce-scatter.2.cloned.1.call-done = f32[128,512]{1,0:T(8,128)} async-done(((f32[8192,512]{1,0:T(8,128)}), f32[128,512]{1,0:T(8,128)}) %reduce-scatter.2.cloned.1.call-update) | async-done | bytes 262160 | tf_op jit(solution)/shard_map/reduce_scatter | solution.py:82
  553.7 0.0 copy-done.5
  553.7 1.1 multiply_reduce_fusion.3
  554.8 1.8 subtract_divide_fusion
  (4 shorter events, 0.0 us)
Async XLA Ops:
  8.0 133.1 %copy-start = (bf16[1408,512]{1,0:T(8,128)(2,1)S(1)}, bf16[1408,512]{1,0:T(8,128)(2,1)}, u32[]{:S(2)}) copy-start(bf16[1408,512]{1,0:T(8,128)(2,1)} %param.10) | copy-start | bytes 4325380
  8.0 131.6 %all-reduce.3.cloned.1.call-start = ((), (), s32[]{:S(2)}) async-start(), calls=%async_computation.1 | async-start | bytes 2883584 | tf_op jit(solution)/shard_map/psum | solution.py:53
  36.5 16.1 %copy-start.7 = (f32[256,16]{1,0:T(8,128)}, f32[256,16]{1,0:T(8,128)S(1)}, u32[]{:S(2)}) copy-start(f32[256,16]{1,0:T(8,128)S(1)} %psum.21) | copy-start | bytes 49156
  79.7 138.3 %all-gather.2.cloned.1.call-start = ((), (), s32[]{:S(2)}) async-start(), calls=%async_computation.2 | async-start | bytes 8519680 | tf_op jit(solution)/shard_map/all_gather | solution.py:70
  82.5 187.8 %all-reduce.5.cloned.1.call-start = ((), (), s32[]{:S(2)}) async-start(), calls=%async_computation.3 | async-start | bytes 524288 | tf_op jit(solution)/shard_map/psum | solution.py:83
  141.8 128.6 %copy-start.3 = (f32[256,512]{1,0:T(8,128)}, f32[256,512]{1,0:T(8,128)S(1)}, u32[]{:S(2)}) copy-start(f32[256,512]{1,0:T(8,128)S(1)} %get-tuple-element.7) | copy-start | bytes 1572868
  218.1 9.7 %copy-start.9 = (bf16[8192,512]{1,0:T(8,128)(2,1)S(1)}, bf16[8192,512]{1,0:T(8,128)(2,1)}, u32[]{:S(2)}) copy-start(bf16[8192,512]{1,0:T(8,128)(2,1)} %all-gather.2.cloned.1.call-done) | copy-start | bytes 25165828
  225.7 2.0 copy-start.4
  230.8 322.9 %reduce-scatter.2.cloned.1.call-start = ((), (), s32[]{:S(2)}) async-start(), calls=%async_computation.4 | async-start | bytes 17039360 | tf_op jit(solution)/shard_map/reduce_scatter | solution.py:82
  271.5 8.9 %copy-start.2 = (f32[256,16,88]{2,1,0:T(8,128)S(1)}, f32[256,16,88]{2,1,0:T(8,128)}, u32[]{:S(2)}) copy-start(f32[256,16,88]{2,1,0:T(8,128)} %copy.21) | copy-start | bytes 4325380
  280.4 7.3 %copy-start.6 = (f32[256,1408]{1,0:T(8,128)S(1)}, f32[256,1408]{1,0:T(8,128)}, u32[]{:S(2)}) copy-start(f32[256,1408]{1,0:T(8,128)} %fusion.27) | copy-start | bytes 4325380
  280.4 7.3 %copy-start.10 = (bf16[1408,1408]{1,0:T(8,128)(2,1)S(1)}, bf16[1408,1408]{1,0:T(8,128)(2,1)}, u32[]{:S(2)}) copy-start(bf16[1408,1408]{1,0:T(8,128)(2,1)} %param.9) | copy-start | bytes 11894788
  287.7 15.5 %copy-start.1 = (f32[256,8,16]{2,1,0:T(8,128)S(1)}, f32[256,8,16]{2,1,0:T(8,128)}, u32[]{:S(2)}) copy-start(f32[256,8,16]{2,1,0:T(8,128)} %get-tuple-element.3) | copy-start | bytes 393220
  287.7 15.5 %copy-start.8 = (bf16[1408,16]{0,1:T(8,128)(2,1)S(1)}, bf16[1408,16]{0,1:T(8,128)(2,1)}, u32[]{:S(2)}) copy-start(bf16[1408,16]{0,1:T(8,128)(2,1)} %param.8) | copy-start | bytes 135172
  303.2 250.4 %copy-start.5 = (bf16[128,512]{1,0:T(8,128)(2,1)S(1)}, bf16[128,512]{1,0:T(8,128)(2,1)}, u32[]{:S(2)}) copy-start(bf16[128,512]{1,0:T(8,128)(2,1)} %param.11) | copy-start | bytes 393220
Sparse Core Ops, SparseCore 0:
  79.9 59.6 all-reduce.2
  230.9 33.0 all-reduce.4
Sparse Core Ops, SparseCore 1:
  82.6 135.4 all-gather.1
  241.3 312.3 reduce-scatter.1
where the time goes:
time: 565 us; the launch traced here: 564 us
  waiting for transfers between devices  373 us (66%)
  matrix products  67.9 us (12%)
  local copies, waits for them, and re-layouts  58.5 us (10%)
  other arithmetic  24.2 us (4%)
  blocking collectives  23.5 us (4%)
  between operations  17 us (3%)
    reduce_scatter x1, waiting for transfers between devices, local(): lax.psum_scatter(text_terms, 'clip', scatter_dimension=0, tiled=True)  242 us
    all_gather x1, waiting for transfers between devices, local(): gathered = lax.all_gather(text_half, 'clip', axis=0, tiled=True)  76.3 us
    psum x1, waiting for transfers between devices, local(): lax.psum((jnp.sum(exponent, axis=1), weighted_values(exponent, values, he...  54.5 us
    another operation x1, local copies, waits for them, and re-layouts, weighted_values(): values.reshape(clip_count, frame_count, head_count, head_size)  18.8 us
    reshape x1, local copies, waits for them, and re-layouts, local(): weight_wide = jnp.repeat(weights, head_size, axis=2)  17.4 us
    dot_general x1, matrix products, local(): lax.dot_general(value_grad, value_weight, (((1,), (1,)), ((), ())), prefe...  15.5 us
    dot_general x1, matrix products, local(): jnp.dot(frame_rows, value_weight, preferred_element_type=jnp.float32)  14.5 us
    pmax x1, blocking collectives, local(): global_max = lax.pmax(local_max, 'tm')  13.8 us
  transfers between devices with their start and end apart: 4, of which 3 were waited for; matrix products, arithmetic and copies ran while one was open for 15% of the time, Pallas kernels for 0%

commit v1 on v0

v1 whole, which is shorter than its diff:
```python
import functools
import math

import jax
import jax.numpy as jnp
from jax import lax
from jax.experimental import pallas as pl
from jax.experimental.pallas import tpu as pltpu
from jax.sharding import PartitionSpec as P

EPSILON = 1e-06
MESH = pl.DeviceIdType.MESH
BF = jnp.bfloat16
F32 = jnp.float32
NT = (((1,), (1,)), ((), ()))
TN = (((0,), (0,)), ((), ()))
HEADS = 16
GROUP = 16


def nt(a, b):
    return lax.dot_general(a, b, NT, preferred_element_type=F32)


def tn(a, b):
    return lax.dot_general(a, b, TN, preferred_element_type=F32)


def nn(a, b):
    return jnp.dot(a, b, preferred_element_type=F32)


def split_nn(a, b):
    high = a.astype(BF)
    low = (a - high.astype(F32)).astype(BF)
    return nn(high, b) + nn(low, b)


def own_clip_mask(rows_per_clip):
    shape = (GROUP * rows_per_clip, HEADS * GROUP)
    row = lax.broadcasted_iota(jnp.int32, shape, 0)
    lane = lax.broadcasted_iota(jnp.int32, shape, 1) & (GROUP - 1)
    start = lane * rows_per_clip
    return jnp.where((row >= start) & (row < start + rows_per_clip), 1.0, 0.0)


def repeat_heads(key_ref, out_ref):
    for h in range(HEADS):
        row = key_ref[h : h + 1, :].astype(F32)
        wide = jnp.broadcast_to(row, (GROUP, row.shape[1])).astype(BF)
        out_ref[h * GROUP : (h + 1) * GROUP, :] = wide


def main_kernel(
    dims,
    frames_hbm, key_hbm, value_hbm, out_hbm, texts_hbm, scale_ref, bias_ref,
    vp_hbm, sg_hbm, gt_hbm,
    key_ref, texts_ref, gt_ref,
    x_s, w_s, ow_s, key_s, pq_s, e_s, ms_send, ms_recv, alpha_s, acc_s, a_s, sg_s, t_s,
    tt_s, tg_s, rsib_s, r1_s, r2_s, tr_s, q1_s, q2_s, g_s,
    embp_s, embr_s, vu_s, vn_s, v_s, vg_s, vgb_s, g1_s, g2_s, eg_s, egr_s, pg_s, u_send, u_recv,
    load_sem, out_sem, send_sem, recv_sem,
):
    clips, width, head, emb, all_clips = dims
    frames_here = 8
    rows = clips * frames_here
    groups = clips // GROUP
    half_clips = clips // 2
    root = 1.0 / math.sqrt(width)

    tm = lax.axis_index("tm")
    ci = lax.axis_index("clip")
    core = lax.rem(ci, 2)
    y = lax.rem(ci // 2, 4)
    x = lax.rem(ci // 8, 4)
    z_lo = ci // 32
    z = tm * 2 + z_lo

    def at(xx, yy, zz, cc):
        return (zz // 2, ((lax.rem(zz, 2) * 4 + xx) * 4 + yy) * 2 + cc)

    def up(a, n):
        return lax.rem(a + n, 4)

    p1 = x * (1 - core) + y * core
    p2 = y * (1 - core) + x * core

    def plane(a1, a2):
        return at(a1 * (1 - core) + a2 * core, a2 * (1 - core) + a1 * core, z, core)

    n1p, n1m = plane(up(p1, 1), p2), plane(up(p1, 3), p2)
    n2p, n2m = plane(p1, up(p2, 1)), plane(p1, up(p2, 3))
    zp, zm = at(x, y, up(z, 1), core), at(x, y, up(z, 3), core)
    partner = (1 - tm, ci)
    sibling = at(x, y, z, 1 - core)

    counter = [0]

    def remote(src, dst, device):
        k = counter[0]
        counter[0] += 1
        return pltpu.make_async_remote_copy(
            src_ref=src, dst_ref=dst, send_sem=send_sem.at[k], recv_sem=recv_sem.at[k],
            device_id=device, device_id_type=MESH,
        )

    chunk = rows // 4
    loads = [
        pltpu.make_async_copy(
            frames_hbm.at[pl.ds(i * chunk, chunk)], x_s.at[pl.ds(i * chunk, chunk)], load_sem.at[i]
        )
        for i in range(4)
    ]
    load_w = pltpu.make_async_copy(value_hbm, w_s, load_sem.at[4])
    load_ow = pltpu.make_async_copy(out_hbm, ow_s, load_sem.at[5])
    load_key = pltpu.make_async_copy(key_hbm, key_ref, load_sem.at[6])
    load_texts = pltpu.make_async_copy(texts_hbm, texts_ref, load_sem.at[7])
    load_texts.start()
    load_key.start()
    for load in loads:
        load.start()
    load_w.start()
    load_ow.start()

    barrier = pltpu.get_barrier_semaphore()
    greet = (n1p, n1m, n2p, n2m, zp, zm, partner, sibling)
    for device in greet:
        pl.semaphore_signal(barrier, inc=1, device_id=device, device_id_type=MESH)

    load_texts.wait()
    text_full = texts_ref[...].astype(F32)
    text_norm = jnp.sqrt(jnp.sum(text_full * text_full, axis=1, keepdims=True) + EPSILON)
    tt_s[1, p2, p1] = (text_full / text_norm).astype(BF)
    load_key.wait()
    repeat_heads(key_ref, key_s)

    pl.semaphore_wait(barrier, len(greet))

    sent = []

    def go(*copies):
        for copy in copies:
            copy.start()
            sent.append(copy)

    own = tt_s.at[1]
    a0p = remote(own.at[p2, p1], own.at[p2, p1], n1p)
    a0m = remote(own.at[p2, p1], own.at[p2, p1], n1m)
    go(a0p, a0m)

    mask = own_clip_mask(frames_here)
    clip_mask = own_clip_mask(1)
    lanes = HEADS * GROUP

    def own_lane(per_clip):
        picked = per_clip.reshape(per_clip.shape[0] // GROUP, GROUP, lanes) * clip_mask[None]
        return jnp.sum(picked, axis=1)

    for i in range(4):
        loads[i].wait()
        part = pl.ds(i * chunk, chunk)
        s = nt(x_s[part, :], key_s[...]) * root
        s3 = s.reshape(chunk // frames_here, frames_here, lanes)
        top = jnp.max(s3, axis=1)
        e3 = jnp.exp(s3 - top[:, None, :])
        e_s[part, :] = e3.reshape(chunk, lanes)
        group_part = pl.ds(i * groups // 4, groups // 4)
        ms_send[0, group_part, :] = own_lane(top)
        ms_send[1, group_part, :] = own_lane(jnp.sum(e3, axis=1))
    ms = remote(ms_send, ms_recv, partner)
    go(ms)

    def a1():
        a0p.wait_recv()
        a0m.wait_recv()
        low, high = pl.ds(0, 64), pl.ds(64, 64)
        b1, b3 = up(p1, 3), up(p1, 1)
        cp = remote(own.at[p2, b1, low], own.at[p2, b1, low], n1p)
        cm = remote(own.at[p2, b3, high], own.at[p2, b3, high], n1m)
        go(cp, cm)
        return cp, cm

    def sib_row(row):
        copy = remote(own.at[row], tt_s.at[0, row], sibling)
        go(copy)
        return copy

    fwd1 = a1()

    columns = [slice(at, min(at + 256, width)) for at in range(0, width, 256)]

    def pool_group(g, carry):
        frame_part = pl.ds(pl.multiple_of(g * 128, 128), 128)
        clip_part = pl.ds(pl.multiple_of(g * GROUP, GROUP), GROUP)
        weight = jnp.transpose(e_s[frame_part, :] * mask).astype(BF)
        for cols in columns:
            pooled = nn(weight, x_s[frame_part, cols]).astype(BF)
            pq_s[:, clip_part, cols] = pooled.reshape(HEADS, GROUP, pooled.shape[1])
        return carry

    lax.fori_loop(0, groups // 2, pool_group, 0, unroll=4)

    for copy in fwd1:
        copy.wait_recv()
    row_p = remote(own.at[p2], own.at[p2], n2p)
    row_m = remote(own.at[p2], own.at[p2], n2m)
    go(row_p, row_m)
    sib0 = sib_row(p2)

    lax.fori_loop(groups // 2, groups, pool_group, 0, unroll=4)

    load_w.wait()
    load_ow.wait()
    acc_s[...] = jnp.zeros_like(acc_s)

    pairs = []
    for h in range(0, HEADS, 2):
        first = min(h * head // 128, width // 128 - 2) * 128
        wide = 256 if (h + 2) * head <= first + 256 else 384
        pairs.append((h, first, wide))

    def window_mask(h, first, wide):
        lane = lax.broadcasted_iota(jnp.int32, (1, wide), 1)
        offset = h * head - first
        return (lane >= offset) & (lane < offset + head)

    for h, first, wide in pairs:
        cols = slice(first, first + wide)
        part = nn(pq_s[h : h + 2].reshape(2 * clips, width), w_s[:, cols])
        acc_s[:, cols] += jnp.where(window_mask(h, first, wide), part[:clips], 0.0) + jnp.where(
            window_mask(h + 1, first, wide), part[clips:], 0.0
        )

    ms.wait_recv()
    mine, theirs = ms_send[0], ms_recv[0]
    top = jnp.maximum(mine, theirs)
    mine_f, theirs_f = jnp.exp(mine - top), jnp.exp(theirs - top)
    alpha = mine_f / (ms_send[1] * mine_f + ms_recv[1] * theirs_f)
    alpha_s[...] = alpha
    spread = (alpha[:, None, :] * clip_mask[None]).reshape(clips, lanes)
    head_start = (lax.broadcasted_iota(jnp.int32, (lanes, width), 0) // GROUP) * head
    head_lane = lax.broadcasted_iota(jnp.int32, (lanes, width), 1)
    in_head = (head_lane >= head_start) & (head_lane < head_start + head)
    pooled = (acc_s[...] * split_nn(spread, jnp.where(in_head, 1.0, 0.0).astype(BF))).astype(BF)
    embp_s[...] = nn(pooled, ow_s[...]).astype(BF).reshape(2, half_clips, emb)
    er_p = remote(embp_s.at[up(z, 1) // 2], embr_s.at[0], zp)
    er_m = remote(embp_s.at[up(z, 3) // 2], embr_s.at[1], zm)
    go(er_p, er_m)

    row_p.wait_recv()
    row_m.wait_recv()
    r1, r3 = up(p2, 3), up(p2, 1)
    low, high = pl.ds(0, 2), pl.ds(2, 2)
    fwd_p = remote(own.at[r1, low], own.at[r1, low], n2p)
    fwd_m = remote(own.at[r3, high], own.at[r3, high], n2m)
    go(fwd_p, fwd_m)
    sib1 = sib_row(r3)
    sib2 = sib_row(r1)

    def weights(g, carry):
        frame_part = pl.ds(pl.multiple_of(g * 128, 128), 128)
        wide = e_s[frame_part, :] * mask * alpha_s[pl.ds(g, 1), :]
        e_s[frame_part, :] = wide
        a_s[frame_part, :] = wide.astype(BF)
        return carry

    lax.fori_loop(0, groups // 2, weights, 0, unroll=4)

    er_p.wait_recv()
    er_m.wait_recv()
    embedding = embr_s[0].astype(F32) + embr_s[1].astype(F32)
    vis_norm = jnp.sqrt(jnp.sum(embedding * embedding, axis=1, keepdims=True) + EPSILON)
    vis_unit = embedding / vis_norm
    vu_s[...] = vis_unit
    vn_s[...] = jnp.broadcast_to(vis_norm, vn_s.shape)
    v_s[z] = vis_unit.astype(BF)
    v_p = remote(v_s.at[z], v_s.at[z], zp)
    v_m = remote(v_s.at[z], v_s.at[z], zm)
    go(v_p, v_m)
    lax.fori_loop(groups // 2, groups, weights, 0, unroll=4)
    v_p.wait_recv()
    v_m.wait_recv()
    z1, z2, z3 = up(z, 1), up(z, 2), up(z, 3)
    hlow, hhigh = pl.ds(0, half_clips // 2), pl.ds(half_clips // 2, half_clips // 2)
    v_fp = remote(v_s.at[z3, hlow], v_s.at[z3, hlow], zp)
    v_fm = remote(v_s.at[z1, hhigh], v_s.at[z1, hhigh], zm)
    go(v_fp, v_fm)

    fwd_p.wait_recv()
    fwd_m.wait_recv()
    sib3 = sib_row(up(p2, 2))
    v_fp.wait_recv()
    v_fm.wait_recv()

    vg_s[...] = jnp.zeros_like(vg_s)
    slope = 0.5 * scale_ref[0]
    shift = 0.5 * bias_ref[0]
    diff = lax.broadcasted_iota(jnp.int32, (128, 128), 0) - lax.broadcasted_iota(
        jnp.int32, (128, 128), 1
    )
    vis_base = [
        (((1 - zz % 2) * 4 + x) * 4 + y) * 2 * clips + core * clips + (zz // 2) * half_clips
        for zz in range(4)
    ]

    def text_base(whose, a2, a1):
        c = core * whose + (1 - core) * (1 - whose)
        xx = a1 * (1 - c) + a2 * c
        yy = a2 * (1 - c) + a1 * c
        return (tm * 64 + ((z_lo * 4 + xx) * 4 + yy) * 2 + c) * 128

    def pair_row(whose, row):
        vis = v_s[...].reshape(4 * half_clips, emb)
        total = None
        for hh in range(2):
            texts = tt_s[whose, row, pl.ds(2 * hh, 2)].reshape(256, emb)
            curve = jnp.tanh(nt(vis, texts) * slope + shift) * 0.5
            tall = []
            for zz in range(4):
                wide = []
                for b in range(2):
                    gap = text_base(whose, row, 2 * hh + b) - vis_base[zz]
                    block = curve[zz * 128 : (zz + 1) * 128, b * 128 : (b + 1) * 128]
                    wide.append(block + jnp.where(diff == gap, -0.5, 0.5))
                tall.append(jnp.concatenate(wide, axis=1))
            grad = jnp.concatenate(tall, axis=0).astype(BF)
            g_s[whose, row, hh] = grad
            part = nn(grad, texts)
            total = part if total is None else total + part
        vg_s[...] += total

    def pair_rows(whose):
        def body(row, carry):
            pair_row(whose, row)
            return carry

        lax.fori_loop(0, 4, body, 0)

    pair_rows(1)
    for copy in (sib0, sib1, sib2, sib3):
        copy.wait_recv()
    pair_rows(0)

    vgb_s[...] = vg_s[...].astype(BF).reshape(4, half_clips, emb)
    g1p = remote(vgb_s.at[z2, hlow], g1_s.at[0], zp)
    g1m = remote(vgb_s.at[z2, hhigh], g1_s.at[1], zm)
    g2p = remote(vgb_s.at[z1, hhigh], g2_s.at[0, hhigh], zp)
    g2m = remote(vgb_s.at[z3, hlow], g2_s.at[1, hlow], zm)
    go(g1p, g1m, g2p, g2m)

    sib_base = counter[0]
    counter[0] += 4

    def sib_copy(rr, row):
        return pltpu.make_async_remote_copy(
            src_ref=tg_s.at[0, row], dst_ref=rsib_s.at[row],
            send_sem=send_sem.at[sib_base + rr], recv_sem=recv_sem.at[sib_base + rr],
            device_id=sibling, device_id_type=MESH,
        )

    def ordered(p, rr):
        return lax.rem(p + 2 + 3 * rr + 3 * (rr // 2) + 2 * (rr // 3), 4)

    def text_terms(whose, row):
        vis = v_s[...].reshape(4 * half_clips, emb)
        grad = jnp.concatenate([g_s[whose, row, 0], g_s[whose, row, 1]], axis=1)
        return tn(grad, vis).reshape(4, 128, emb)

    def sib_rows(rr, carry):
        row = ordered(p1, rr)
        tg_s[0, row] = text_terms(0, row).astype(BF)
        sib_copy(rr, row).start()
        return carry

    lax.fori_loop(0, 4, sib_rows, 0)

    g1p.wait_recv()
    g1m.wait_recv()
    vgb_s[z1, hlow] = (vgb_s[z1, hlow].astype(F32) + g1_s[0].astype(F32)).astype(BF)
    g3p = remote(vgb_s.at[z1, hlow], g2_s.at[0, hlow], zp)
    vgb_s[z3, hhigh] = (vgb_s[z3, hhigh].astype(F32) + g1_s[1].astype(F32)).astype(BF)
    g3m = remote(vgb_s.at[z3, hhigh], g2_s.at[1, hhigh], zm)
    go(g3p, g3m)

    def own_rows(rr, carry):
        row = ordered(p2, rr)
        sib_copy(rr, row).wait_recv()
        tg_s[1, row] = (text_terms(1, row) + rsib_s[row].astype(F32)).astype(BF)
        return carry

    tg = tg_s.at[1]
    lax.fori_loop(0, 1, own_rows, 0)
    s1p = remote(tg.at[up(p2, 2), low], r1_s.at[0], n2p)
    s1m = remote(tg.at[up(p2, 2), high], r1_s.at[1], n2m)
    go(s1p, s1m)
    lax.fori_loop(1, 2, own_rows, 0)
    s2p = remote(tg.at[r3, high], r2_s.at[0, high], n2p)
    go(s2p)
    lax.fori_loop(2, 3, own_rows, 0)
    s2m = remote(tg.at[r1, low], r2_s.at[1, low], n2m)
    go(s2m)

    for copy in (g2p, g2m, g3p, g3m):
        copy.wait_recv()
    out_scale = scale_ref[0] * (1.0 / all_clips)
    vis_grad = (
        vg_s[pl.ds(pl.multiple_of(z * half_clips, 128), half_clips), :]
        + g2_s[0].astype(F32)
        + g2_s[1].astype(F32)
    ) * out_scale
    unit = vu_s[...]
    inner = jnp.sum(vis_grad * unit, axis=1, keepdims=True)
    eg_s[...] = ((vis_grad - unit * inner) / vn_s[:, :1]).astype(BF)
    eg_p = remote(eg_s, egr_s.at[tm], zp)
    eg_m = remote(eg_s, egr_s.at[tm], zm)
    go(eg_p, eg_m)

    lax.fori_loop(3, 4, own_rows, 0)
    s1p.wait_recv()
    s1m.wait_recv()
    tg_s[1, r3, low] = (tg_s[1, r3, low].astype(F32) + r1_s[0].astype(F32)).astype(BF)
    s3p = remote(tg.at[r3, low], r2_s.at[0, low], n2p)
    go(s3p)
    tg_s[1, r1, high] = (tg_s[1, r1, high].astype(F32) + r1_s[1].astype(F32)).astype(BF)
    s3m = remote(tg.at[r1, high], r2_s.at[1, high], n2m)
    go(s3m)

    eg_p.wait_recv()
    eg_m.wait_recv()
    pg_s[...] = nt(egr_s[...].reshape(clips, emb), ow_s[...]).astype(BF)

    for h, first, wide in pairs:
        grads = pg_s[:, first : first + wide].astype(F32)
        part = jnp.concatenate(
            [jnp.where(window_mask(h + i, first, wide), grads, 0.0).astype(BF) for i in range(2)],
            axis=0,
        )
        for cols in columns:
            q = nt(part, w_s[cols, first : first + wide]).astype(BF)
            pq_s[h : h + 2, :, cols] = q.reshape(2, clips, q.shape[1])

    def score_terms(g, carry):
        frame_part = pl.ds(pl.multiple_of(g * 128, 128), 128)
        clip_part = pl.ds(pl.multiple_of(g * GROUP, GROUP), GROUP)
        q = pq_s[:, clip_part, :].reshape(lanes, width)
        prod = jnp.transpose(nt(q, x_s[frame_part, :]))
        t_s[frame_part, :] = prod
        u_send[pl.ds(g, 1), :] = jnp.sum(prod * e_s[frame_part, :], axis=0, keepdims=True)
        return carry

    lax.fori_loop(0, groups, score_terms, 0, unroll=4)
    uc = remote(u_send, u_recv, partner)
    uc.start()

    for copy in (s2p, s2m, s3p, s3m):
        copy.wait_recv()
    for b in range(4):
        total = tg_s[1, p2, b].astype(F32) + r2_s[0, b].astype(F32) + r2_s[1, b].astype(F32)
        tr_s[b] = total.astype(BF)
    b1, b2, b3 = up(p1, 1), up(p1, 2), up(p1, 3)
    tlow, thigh = pl.ds(0, 64), pl.ds(64, 64)
    u1p = remote(tr_s.at[b2, tlow], q1_s.at[0], n1p)
    u1m = remote(tr_s.at[b2, thigh], q1_s.at[1], n1m)
    u2p = remote(tr_s.at[b1, thigh], q2_s.at[0, thigh], n1p)
    u2m = remote(tr_s.at[b3, tlow], q2_s.at[1, tlow], n1m)
    go(u1p, u1m, u2p, u2m)

    def vp_copy(g):
        frame_part = pl.ds(pl.multiple_of(g * 128, 128), 128)
        return pltpu.make_async_copy(
            x_s.at[frame_part], vp_hbm.at[frame_part], out_sem.at[g]
        )

    def value_part(g, carry):
        frame_part = pl.ds(pl.multiple_of(g * 128, 128), 128)
        clip_part = pl.ds(pl.multiple_of(g * GROUP, GROUP), GROUP)
        for cols in columns:
            q = pq_s[:, clip_part, cols]
            q = q.reshape(lanes, q.shape[2])
            x_s[frame_part, cols] = nn(a_s[frame_part, :], q).astype(BF)
        vp_copy(g).start()
        return carry

    lax.fori_loop(0, groups // 2, value_part, 0, unroll=4)
    u1p.wait_recv()
    u1m.wait_recv()
    tr_s[b1, tlow] = (tr_s[b1, tlow].astype(F32) + q1_s[0].astype(F32)).astype(BF)
    u3p = remote(tr_s.at[b1, tlow], q2_s.at[0, tlow], n1p)
    tr_s[b3, thigh] = (tr_s[b3, thigh].astype(F32) + q1_s[1].astype(F32)).astype(BF)
    u3m = remote(tr_s.at[b3, thigh], q2_s.at[1, thigh], n1m)
    go(u3p, u3m)

    lax.fori_loop(groups // 2, groups, value_part, 0, unroll=4)

    for copy in (u2p, u2m, u3p, u3m):
        copy.wait_recv()
    gt_ref[...] = (
        tr_s[p1].astype(F32) + q2_s[0].astype(F32) + q2_s[1].astype(F32)
    ) * out_scale
    gt_out = pltpu.make_async_copy(gt_ref, gt_hbm, load_sem.at[8])
    gt_out.start()

    uc.wait()
    u_send[...] = u_send[...] + u_recv[...]

    def score_grads(g, carry):
        frame_part = pl.ds(pl.multiple_of(g * 128, 128), 128)
        centred = t_s[frame_part, :] - u_send[pl.ds(g, 1), :]
        sg_s[frame_part, :] = (e_s[frame_part, :] * centred * root).astype(BF)
        return carry

    sg_out = []
    for i in range(2):
        lax.fori_loop(i * groups // 2, (i + 1) * groups // 2, score_grads, 0, unroll=4)
        part = pl.ds(i * rows // 2, rows // 2)
        sg_out.append(pltpu.make_async_copy(sg_s.at[part], sg_hbm.at[part], load_sem.at[9 + i]))
        sg_out[i].start()

    for copy in sent:
        copy.wait_send()

    def drain(rr, carry):
        sib_copy(rr, ordered(p1, rr)).wait_send()
        return carry

    lax.fori_loop(0, 4, drain, 0)

    def drain_vp(g, carry):
        vp_copy(g).wait()
        return carry

    lax.fori_loop(0, groups, drain_vp, 0)
    for copy in sg_out:
        copy.wait()
    gt_out.wait()


def final_kernel(
    vp_hbm, sg_hbm, key_hbm, texts_hbm, tg_hbm, out_hbm, gt_hbm,
    vp_s, sg_s, key_in, key_s, texts_s, tg_s, gt_s, vp_sem, sg_sem, out_sem, small_sem,
):
    rows, width = vp_s.shape
    steps = 8
    step = rows // steps
    parts = [pl.ds(i * step, step) for i in range(steps)]
    load_key = pltpu.make_async_copy(key_hbm, key_in, small_sem.at[0])
    load_texts = pltpu.make_async_copy(texts_hbm, texts_s, small_sem.at[1])
    load_tg = pltpu.make_async_copy(tg_hbm, tg_s, small_sem.at[2])
    load_key.start()
    load_vp, load_sg, outs = [], [], []
    for i, part in enumerate(parts):
        load_sg.append(pltpu.make_async_copy(sg_hbm.at[part], sg_s.at[part], sg_sem.at[i]))
        load_vp.append(pltpu.make_async_copy(vp_hbm.at[part], vp_s.at[part], vp_sem.at[i]))
        outs.append(pltpu.make_async_copy(vp_s.at[part], out_hbm.at[part], out_sem.at[i]))
        load_sg[i].start()
        load_vp[i].start()
        if i == 1:
            load_texts.start()
            load_tg.start()
    load_key.wait()
    repeat_heads(key_in, key_s)
    for i, part in enumerate(parts):
        load_sg[i].wait()
        load_vp[i].wait()
        for start in range(0, width, 256):
            cols = slice(start, min(start + 256, width))
            total = vp_s[part, cols].astype(F32) + nn(sg_s[part, :], key_s[:, cols])
            vp_s[part, cols] = total.astype(BF)
        outs[i].start()
        if i == 2:
            load_texts.wait()
            load_tg.wait()
            text_full = texts_s[...].astype(F32)
            text_norm = jnp.sqrt(jnp.sum(text_full * text_full, axis=1, keepdims=True) + EPSILON)
            text_unit = text_full / text_norm
            text_grad = tg_s[...]
            inner = jnp.sum(text_grad * text_unit, axis=1, keepdims=True)
            gt_s[...] = (text_grad - text_unit * inner) / text_norm
            gt_out = pltpu.make_async_copy(gt_s, gt_hbm, small_sem.at[3])
            gt_out.start()
    for copy in outs:
        copy.wait()
    gt_out.wait()


def local(frames, key_proj, value_weight, out_weight, texts, logit_scale, logit_bias):
    clips, frames_here, width = frames.shape
    heads = key_proj.shape[1]
    head = width // heads
    emb = out_weight.shape[1]
    all_clips = clips * lax.axis_size("clip")
    rows = clips * frames_here
    half = clips // 2
    frame_rows = frames.reshape(rows, width)
    key_t = key_proj.T
    V = pltpu.VMEM
    copies = 48
    scratch = [
        V((heads, width), BF),
        V((128, emb), BF),
        V((128, emb), F32),
        V((rows, width), BF),
        V((width, width), BF),
        V((width, emb), BF),
        V((heads * GROUP, width), BF),
        V((heads, clips, width), BF),
        V((rows, heads * GROUP), F32),
        V((2, clips // GROUP, heads * GROUP), F32),
        V((2, clips // GROUP, heads * GROUP), F32),
        V((clips // GROUP, heads * GROUP), F32),
        V((clips, width), F32),
        V((rows, heads * GROUP), BF),
        V((rows, heads * GROUP), BF),
        V((rows, heads * GROUP), F32),
        V((2, 4, 4, 128, emb), BF),
        V((2, 4, 4, 128, emb), BF),
        V((4, 4, 128, emb), BF),
        V((2, 2, 128, emb), BF),
        V((2, 4, 128, emb), BF),
        V((4, 128, emb), BF),
        V((2, 64, emb), BF),
        V((2, 128, emb), BF),
        V((2, 4, 2, 4 * half, 256), BF),
        V((2, half, emb), BF),
        V((2, half, emb), BF),
        V((half, emb), F32),
        V((half, 128), F32),
        V((4, half, emb), BF),
        V((4 * half, emb), F32),
        V((4, half, emb), BF),
        V((2, half // 2, emb), BF),
        V((2, half, emb), BF),
        V((half, emb), BF),
        V((2, half, emb), BF),
        V((clips, width), BF),
        V((clips // GROUP, heads * GROUP), F32),
        V((clips // GROUP, heads * GROUP), F32),
        pltpu.SemaphoreType.DMA((11,)),
        pltpu.SemaphoreType.DMA((clips // GROUP,)),
        pltpu.SemaphoreType.DMA((copies,)),
        pltpu.SemaphoreType.DMA((copies,)),
    ]
    anywhere = pl.BlockSpec(memory_space=pl.ANY)
    smem = pl.BlockSpec(memory_space=pltpu.SMEM)
    value_part, score_grad, text_grad = pl.pallas_call(
        functools.partial(main_kernel, (clips, width, head, emb, all_clips)),
        out_shape=(
            jax.ShapeDtypeStruct((rows, width), BF),
            jax.ShapeDtypeStruct((rows, heads * GROUP), BF),
            jax.ShapeDtypeStruct((128, emb), F32),
        ),
        in_specs=[anywhere] * 5 + [smem] * 2,
        out_specs=(anywhere, anywhere, anywhere),
        scratch_shapes=scratch,
        compiler_params=pltpu.CompilerParams(
            collective_id=0, has_side_effects=True, vmem_limit_bytes=60 * 1024 * 1024
        ),
        name="pool_pair_back",
    )(frame_rows, key_t, value_weight, out_weight, texts, logit_scale, logit_bias)
    steps = 8
    grad_frames, grad_texts = pl.pallas_call(
        final_kernel,
        in_specs=[anywhere] * 5,
        out_specs=(anywhere, anywhere),
        out_shape=(
            jax.ShapeDtypeStruct((rows, width), BF),
            jax.ShapeDtypeStruct((128, emb), F32),
        ),
        scratch_shapes=[
            V((rows, width), BF),
            V((rows, heads * GROUP), BF),
            V((heads, width), BF),
            V((heads * GROUP, width), BF),
            V((128, emb), BF),
            V((128, emb), F32),
            V((128, emb), F32),
            pltpu.SemaphoreType.DMA((steps,)),
            pltpu.SemaphoreType.DMA((steps,)),
            pltpu.SemaphoreType.DMA((steps,)),
            pltpu.SemaphoreType.DMA((4,)),
        ],
        compiler_params=pltpu.CompilerParams(vmem_limit_bytes=60 * 1024 * 1024),
        name="frame_grads",
    )(value_part, score_grad, key_t, texts, text_grad)
    return (grad_frames.reshape(clips, frames_here, width), grad_texts)


def solution(mesh):
    in_specs = (P("clip", "tm", None), P(), P(), P(), P(("tm", "clip"), None), P(), P())
    out_specs = (P("clip", "tm", None), P(("tm", "clip"), None))
    return jax.shard_map(local, mesh=mesh, in_specs=in_specs, out_specs=out_specs, check_vma=False)
```

time: 565 us -> 83.7 us (0.15)
  waiting for transfers between devices: 373 us -> 0 us
  Pallas kernels: 0 us -> 81.4 us
  matrix products: 67.9 us -> 0 us
  local copies, waits for them, and re-layouts: 58.5 us -> 0 us
  other arithmetic: 24.2 us -> 0 us
  blocking collectives: 23.5 us -> 0 us
  between operations: 17 us -> 2.09 us
    reduce_scatter x1 -> x0, waiting for transfers between devices: 242 us -> none  [local(): lax.psum_scatter(text_terms, 'clip', scatter_dimension=0, tiled=True)]
    pallas_call x0 -> x2, Pallas kernels: none -> 81.4 us  [the longest x1 74.9 us: local(): pl.pallas_call(functools.partial(main_kernel, (clips, width, head, emb, a...]
    all_gather x1 -> x0, waiting for transfers between devices: 76.3 us -> none  [local(): gathered = lax.all_gather(text_half, 'clip', axis=0, tiled=True)]
    dot_general x9 -> x0, matrix products: 67.9 us -> none  [the longest x1 15.5 us: local(): lax.dot_general(value_grad, value_weight, (((1,), (1,)), ((), ())), prefe...]
    psum x2 -> x0, waiting for transfers between devices: 54.5 us -> none  [the longest x1 54.5 us: local(): lax.psum((jnp.sum(exponent, axis=1), weighted_values(exponent, values, he...]
    another operation x1 -> x0, local copies, waits for them, and re-layouts: 18.8 us -> none  [weighted_values(): values.reshape(clip_count, frame_count, head_count, head_size)]
    reshape x1 -> x0, local copies, waits for them, and re-layouts: 17.4 us -> none  [local(): weight_wide = jnp.repeat(weights, head_size, axis=2)]
    pmax x1 -> x0, blocking collectives: 13.8 us -> none  [local(): global_max = lax.pmax(local_max, 'tm')]
  transfers between devices with their start and end apart: 4 -> 0, of which waited for: 3 -> 0; matrix products, arithmetic and copies ran while one was open for 15% -> 0% of each run, Pallas kernels for 0% -> 0%
where the time goes in v1:
time: 83.7 us; the launch traced here: 83.5 us
  Pallas kernels  81.4 us (97%)
  between operations  2.09 us (2%)
    pallas_call x1, Pallas kernels, local(): pl.pallas_call(functools.partial(main_kernel, (clips, width, head, emb, a...  74.9 us
    pallas_call x1, Pallas kernels, local(): pl.pallas_call(final_kernel, in_specs=[anywhere] * 5, out_specs=(anywhere...  6.5 us

profile of v1, /device:TPU:0, one launch (start us, length us, event | category | flops | bytes accessed | tf_op | source)
XLA Modules:
  0.0 83.5 jit_solution(645208858268219473)
XLA Ops:
  1.9 74.9 %pool_pair_back.1 = (bf16[2048,1408]{1,0:T(8,128)(2,1)}, bf16[2048,256]{1,0:T(8,128)(2,1)}, f32[128,512]{1,0:T(8,128)}) custom-call(bf16[2048,1408]{1,0:T(8,128)(2,1)} %bitcast.3, bf16[16,1408]{1,0:T(8,128)(2,1)} %bitcast.4, bf16[1408,1408]{1,0:T(8,128)(2,1)} %value_hbm.1, bf16[1408,512]{1,0:T(8,128)(2,1)} %out_hbm.1, bf16[128,512]{1,0:T(8,128)(2,1)} %texts_hbm.3, ...), custom_call_target="tpu_custom_call" | custom-call | tf_op jit(solution)/shard_map/pool_pair_back/pallas_call | solution.py:645
  76.9 6.5 %frame_grads.1 = (bf16[2048,1408]{1,0:T(8,128)(2,1)}, f32[128,512]{1,0:T(8,128)}) custom-call(bf16[2048,1408]{1,0:T(8,128)(2,1)} %get-tuple-element.7.vp_hbm, bf16[2048,256]{1,0:T(8,128)(2,1)} %get-tuple-element.8.sg_hbm, bf16[16,1408]{1,0:T(8,128)(2,1)} %bitcast.5, bf16[128,512]{1,0:T(8,128)(2,1)} %texts_hbm.3, f32[128,512]{1,0:T(8,128)} %get-tuple-element.9.tg_hbm), custom_call_target="tpu_custom_call" | custom-call | tf_op jit(solution)/shard_map/frame_grads/pallas_call | solution.py:661

commit v2 on v1

--- a/solution.py
+++ b/solution.py
@@ -82,11 +82,10 @@
     def up(a, n):
         return lax.rem(a + n, 4)
 
-    p1 = x * (1 - core) + y * core
-    p2 = y * (1 - core) + x * core
+    p1, p2 = y, x
 
     def plane(a1, a2):
-        return at(a1 * (1 - core) + a2 * core, a2 * (1 - core) + a1 * core, z, core)
+        return at(a2, a1, z, core)
 
     n1p, n1m = plane(up(p1, 1), p2), plane(up(p1, 3), p2)
     n2p, n2m = plane(p1, up(p2, 1)), plane(p1, up(p2, 3))
@@ -274,23 +273,26 @@
     vu_s[...] = vis_unit
     vn_s[...] = jnp.broadcast_to(vis_norm, vn_s.shape)
     v_s[z] = vis_unit.astype(BF)
-    v_p = remote(v_s.at[z], v_s.at[z], zp)
-    v_m = remote(v_s.at[z], v_s.at[z], zm)
-    go(v_p, v_m)
+    hlow, hhigh = pl.ds(0, half_clips // 2), pl.ds(half_clips // 2, half_clips // 2)
+
+    def send_vis(at_z, half, device):
+        copy = remote(v_s.at[at_z, half], v_s.at[at_z, half], device)
+        go(copy)
+        return copy
+
+    v_first = send_vis(z, hlow, zp), send_vis(z, hhigh, zm)
+    v_second = send_vis(z, hhigh, zp), send_vis(z, hlow, zm)
     lax.fori_loop(groups // 2, groups, weights, 0, unroll=4)
-    v_p.wait_recv()
-    v_m.wait_recv()
     z1, z2, z3 = up(z, 1), up(z, 2), up(z, 3)
-    hlow, hhigh = pl.ds(0, half_clips // 2), pl.ds(half_clips // 2, half_clips // 2)
-    v_fp = remote(v_s.at[z3, hlow], v_s.at[z3, hlow], zp)
-    v_fm = remote(v_s.at[z1, hhigh], v_s.at[z1, hhigh], zm)
-    go(v_fp, v_fm)
+    for copy in v_first:
+        copy.wait_recv()
+    v_far = send_vis(z3, hlow, zp), send_vis(z1, hhigh, zm)
 
     fwd_p.wait_recv()
     fwd_m.wait_recv()
     sib3 = sib_row(up(p2, 2))
-    v_fp.wait_recv()
-    v_fm.wait_recv()
+    for copy in v_second + v_far:
+        copy.wait_recv()
 
     vg_s[...] = jnp.zeros_like(vg_s)
     slope = 0.5 * scale_ref[0]
@@ -305,9 +307,7 @@
 
     def text_base(whose, a2, a1):
         c = core * whose + (1 - core) * (1 - whose)
-        xx = a1 * (1 - c) + a2 * c
-        yy = a2 * (1 - c) + a1 * c
-        return (tm * 64 + ((z_lo * 4 + xx) * 4 + yy) * 2 + c) * 128
+        return (tm * 64 + ((z_lo * 4 + a2) * 4 + a1) * 2 + c) * 128
 
     def pair_row(whose, row):
         vis = v_s[...].reshape(4 * half_clips, emb)
@@ -367,7 +367,7 @@
         return tn(grad, vis).reshape(4, 128, emb)
 
     def sib_rows(rr, carry):
-        row = ordered(p1, rr)
+        row = ordered(p2, rr)
         tg_s[0, row] = text_terms(0, row).astype(BF)
         sib_copy(rr, row).start()
         return carry
@@ -520,7 +520,7 @@
         copy.wait_send()
 
     def drain(rr, carry):
-        sib_copy(rr, ordered(p1, rr)).wait_send()
+        sib_copy(rr, ordered(p2, rr)).wait_send()
         return carry
 
     lax.fori_loop(0, 4, drain, 0)

time: 83.7 us -> 85 us (1.016)
  Pallas kernels: 81.4 us -> 82.8 us
    pallas_call x1, Pallas kernels: 74.9 us -> 76.3 us  [local(): pl.pallas_call(functools.partial(main_kernel, (clips, width, head, emb, a...]
where the time goes in v2:
time: 85 us; the launch traced here: 84.9 us
  Pallas kernels  82.8 us (97%)
  between operations  2.09 us (2%)
    pallas_call x1, Pallas kernels, local(): pl.pallas_call(functools.partial(main_kernel, (clips, width, head, emb, a...  76.3 us
    pallas_call x1, Pallas kernels, local(): pl.pallas_call(final_kernel, in_specs=[anywhere] * 5, out_specs=(anywhere...  6.5 us

profile of v2, /device:TPU:0, one launch (start us, length us, event | category | flops | bytes accessed | tf_op | source)
XLA Modules:
  0.0 84.9 jit_solution(11274496288527938768)
XLA Ops:
  1.9 76.3 %pool_pair_back.1 = (bf16[2048,1408]{1,0:T(8,128)(2,1)}, bf16[2048,256]{1,0:T(8,128)(2,1)}, f32[128,512]{1,0:T(8,128)}) custom-call(bf16[2048,1408]{1,0:T(8,128)(2,1)} %bitcast.3, bf16[16,1408]{1,0:T(8,128)(2,1)} %bitcast.4, bf16[1408,1408]{1,0:T(8,128)(2,1)} %value_hbm.1, bf16[1408,512]{1,0:T(8,128)(2,1)} %out_hbm.1, bf16[128,512]{1,0:T(8,128)(2,1)} %texts_hbm.3, ...), custom_call_target="tpu_custom_call" | custom-call | tf_op jit(solution)/shard_map/pool_pair_back/pallas_call | solution.py:645
  78.2 6.5 %frame_grads.1 = (bf16[2048,1408]{1,0:T(8,128)(2,1)}, f32[128,512]{1,0:T(8,128)}) custom-call(bf16[2048,1408]{1,0:T(8,128)(2,1)} %get-tuple-element.7.vp_hbm, bf16[2048,256]{1,0:T(8,128)(2,1)} %get-tuple-element.8.sg_hbm, bf16[16,1408]{1,0:T(8,128)(2,1)} %bitcast.5, bf16[128,512]{1,0:T(8,128)(2,1)} %texts_hbm.3, f32[128,512]{1,0:T(8,128)} %get-tuple-element.9.tg_hbm), custom_call_target="tpu_custom_call" | custom-call | tf_op jit(solution)/shard_map/frame_grads/pallas_call | solution.py:661

commit v3 on v2

--- a/solution.py
+++ b/solution.py
@@ -28,12 +28,6 @@
 
 def nn(a, b):
     return jnp.dot(a, b, preferred_element_type=F32)
-
-
-def split_nn(a, b):
-    high = a.astype(BF)
-    low = (a - high.astype(F32)).astype(BF)
-    return nn(high, b) + nn(low, b)
 
 
 def own_clip_mask(rows_per_clip):
@@ -82,10 +76,11 @@
     def up(a, n):
         return lax.rem(a + n, 4)
 
-    p1, p2 = y, x
+    p1 = x * (1 - core) + y * core
+    p2 = y * (1 - core) + x * core
 
     def plane(a1, a2):
-        return at(a2, a1, z, core)
+        return at(a1 * (1 - core) + a2 * core, a2 * (1 - core) + a1 * core, z, core)
 
     n1p, n1m = plane(up(p1, 1), p2), plane(up(p1, 3), p2)
     n2p, n2m = plane(p1, up(p2, 1)), plane(p1, up(p2, 3))
@@ -240,7 +235,7 @@
     head_start = (lax.broadcasted_iota(jnp.int32, (lanes, width), 0) // GROUP) * head
     head_lane = lax.broadcasted_iota(jnp.int32, (lanes, width), 1)
     in_head = (head_lane >= head_start) & (head_lane < head_start + head)
-    pooled = (acc_s[...] * split_nn(spread, jnp.where(in_head, 1.0, 0.0).astype(BF))).astype(BF)
+    pooled = (acc_s[...] * nn(spread.astype(BF), jnp.where(in_head, 1.0, 0.0).astype(BF))).astype(BF)
     embp_s[...] = nn(pooled, ow_s[...]).astype(BF).reshape(2, half_clips, emb)
     er_p = remote(embp_s.at[up(z, 1) // 2], embr_s.at[0], zp)
     er_m = remote(embp_s.at[up(z, 3) // 2], embr_s.at[1], zm)
@@ -307,7 +302,9 @@
 
     def text_base(whose, a2, a1):
         c = core * whose + (1 - core) * (1 - whose)
-        return (tm * 64 + ((z_lo * 4 + a2) * 4 + a1) * 2 + c) * 128
+        xx = a1 * (1 - c) + a2 * c
+        yy = a2 * (1 - c) + a1 * c
+        return (tm * 64 + ((z_lo * 4 + xx) * 4 + yy) * 2 + c) * 128
 
     def pair_row(whose, row):
         vis = v_s[...].reshape(4 * half_clips, emb)
@@ -367,7 +364,7 @@
         return tn(grad, vis).reshape(4, 128, emb)
 
     def sib_rows(rr, carry):
-        row = ordered(p2, rr)
+        row = ordered(p1, rr)
         tg_s[0, row] = text_terms(0, row).astype(BF)
         sib_copy(rr, row).start()
         return carry
@@ -416,20 +413,21 @@
     go(eg_p, eg_m)
 
     lax.fori_loop(3, 4, own_rows, 0)
-    s1p.wait_recv()
-    s1m.wait_recv()
-    tg_s[1, r3, low] = (tg_s[1, r3, low].astype(F32) + r1_s[0].astype(F32)).astype(BF)
-    s3p = remote(tg.at[r3, low], r2_s.at[0, low], n2p)
-    go(s3p)
-    tg_s[1, r1, high] = (tg_s[1, r1, high].astype(F32) + r1_s[1].astype(F32)).astype(BF)
-    s3m = remote(tg.at[r1, high], r2_s.at[1, high], n2m)
-    go(s3m)
-
     eg_p.wait_recv()
     eg_m.wait_recv()
     pg_s[...] = nt(egr_s[...].reshape(clips, emb), ow_s[...]).astype(BF)
 
     for h, first, wide in pairs:
+        if h == HEADS // 2:
+            s1p.wait_recv()
+            s1m.wait_recv()
+            tg_s[1, r3, low] = (tg_s[1, r3, low].astype(F32) + r1_s[0].astype(F32)).astype(BF)
+            s3p = remote(tg.at[r3, low], r2_s.at[0, low], n2p)
+            go(s3p)
+            tg_s[1, r1, high] = (tg_s[1, r1, high].astype(F32) + r1_s[1].astype(F32)).astype(BF)
+            s3m = remote(tg.at[r1, high], r2_s.at[1, high], n2m)
+            go(s3m)
+
         grads = pg_s[:, first : first + wide].astype(F32)
         part = jnp.concatenate(
             [jnp.where(window_mask(h + i, first, wide), grads, 0.0).astype(BF) for i in range(2)],
@@ -451,6 +449,24 @@
     lax.fori_loop(0, groups, score_terms, 0, unroll=4)
     uc = remote(u_send, u_recv, partner)
     uc.start()
+
+    def vp_copy(g):
+        frame_part = pl.ds(pl.multiple_of(g * 128, 128), 128)
+        return pltpu.make_async_copy(
+            x_s.at[frame_part], vp_hbm.at[frame_part], out_sem.at[g]
+        )
+
+    def value_part(g, carry):
+        frame_part = pl.ds(pl.multiple_of(g * 128, 128), 128)
+        clip_part = pl.ds(pl.multiple_of(g * GROUP, GROUP), GROUP)
+        for cols in columns:
+            q = pq_s[:, clip_part, cols]
+            q = q.reshape(lanes, q.shape[2])
+            x_s[frame_part, cols] = nn(a_s[frame_part, :], q).astype(BF)
+        vp_copy(g).start()
+        return carry
+
+    lax.fori_loop(0, groups // 4, value_part, 0, unroll=4)
 
     for copy in (s2p, s2m, s3p, s3m):
         copy.wait_recv()
@@ -465,23 +481,7 @@
     u2m = remote(tr_s.at[b3, tlow], q2_s.at[1, tlow], n1m)
     go(u1p, u1m, u2p, u2m)
 
-    def vp_copy(g):
-        frame_part = pl.ds(pl.multiple_of(g * 128, 128), 128)
-        return pltpu.make_async_copy(
-            x_s.at[frame_part], vp_hbm.at[frame_part], out_sem.at[g]
-        )
-
-    def value_part(g, carry):
-        frame_part = pl.ds(pl.multiple_of(g * 128, 128), 128)
-        clip_part = pl.ds(pl.multiple_of(g * GROUP, GROUP), GROUP)
-        for cols in columns:
-            q = pq_s[:, clip_part, cols]
-            q = q.reshape(lanes, q.shape[2])
-            x_s[frame_part, cols] = nn(a_s[frame_part, :], q).astype(BF)
-        vp_copy(g).start()
-        return carry
-
-    lax.fori_loop(0, groups // 2, value_part, 0, unroll=4)
+    lax.fori_loop(groups // 4, 3 * groups // 4, value_part, 0, unroll=4)
     u1p.wait_recv()
     u1m.wait_recv()
     tr_s[b1, tlow] = (tr_s[b1, tlow].astype(F32) + q1_s[0].astype(F32)).astype(BF)
@@ -490,7 +490,23 @@
     u3m = remote(tr_s.at[b3, thigh], q2_s.at[1, thigh], n1m)
     go(u3p, u3m)
 
-    lax.fori_loop(groups // 2, groups, value_part, 0, unroll=4)
+    lax.fori_loop(3 * groups // 4, groups, value_part, 0, unroll=4)
+
+    uc.wait()
+    u_send[...] = u_send[...] + u_recv[...]
+
+    def score_grads(g, carry):
+        frame_part = pl.ds(pl.multiple_of(g * 128, 128), 128)
+        centred = t_s[frame_part, :] - u_send[pl.ds(g, 1), :]
+        sg_s[frame_part, :] = (e_s[frame_part, :] * centred * root).astype(BF)
+        return carry
+
+    sg_out = []
+    for i in range(2):
+        lax.fori_loop(i * groups // 2, (i + 1) * groups // 2, score_grads, 0, unroll=4)
+        part = pl.ds(i * rows // 2, rows // 2)
+        sg_out.append(pltpu.make_async_copy(sg_s.at[part], sg_hbm.at[part], load_sem.at[9 + i]))
+        sg_out[i].start()
 
     for copy in (u2p, u2m, u3p, u3m):
         copy.wait_recv()
@@ -500,27 +516,11 @@
     gt_out = pltpu.make_async_copy(gt_ref, gt_hbm, load_sem.at[8])
     gt_out.start()
 
-    uc.wait()
-    u_send[...] = u_send[...] + u_recv[...]
-
-    def score_grads(g, carry):
-        frame_part = pl.ds(pl.multiple_of(g * 128, 128), 128)
-        centred = t_s[frame_part, :] - u_send[pl.ds(g, 1), :]
-        sg_s[frame_part, :] = (e_s[frame_part, :] * centred * root).astype(BF)
-        return carry
-
-    sg_out = []
-    for i in range(2):
-        lax.fori_loop(i * groups // 2, (i + 1) * groups // 2, score_grads, 0, unroll=4)
-        part = pl.ds(i * rows // 2, rows // 2)
-        sg_out.append(pltpu.make_async_copy(sg_s.at[part], sg_hbm.at[part], load_sem.at[9 + i]))
-        sg_out[i].start()
-
     for copy in sent:
         copy.wait_send()
 
     def drain(rr, carry):
-        sib_copy(rr, ordered(p2, rr)).wait_send()
+        sib_copy(rr, ordered(p1, rr)).wait_send()
         return carry
 
     lax.fori_loop(0, 4, drain, 0)

time: 85 us -> 83.1 us (0.978)
  Pallas kernels: 82.8 us -> 80.9 us
    pallas_call x1, Pallas kernels: 76.3 us -> 74.4 us  [local(): pl.pallas_call(functools.partial(main_kernel, (clips, width, head, emb, a...]
where the time goes in v3:
time: 83.1 us; the launch traced here: 83 us
  Pallas kernels  80.9 us (97%)
  between operations  2.09 us (3%)
    pallas_call x1, Pallas kernels, local(): pl.pallas_call(functools.partial(main_kernel, (clips, width, head, emb, a...  74.4 us
    pallas_call x1, Pallas kernels, local(): pl.pallas_call(final_kernel, in_specs=[anywhere] * 5, out_specs=(anywhere...  6.5 us

profile of v3, /device:TPU:0, one launch (start us, length us, event | category | flops | bytes accessed | tf_op | source)
XLA Modules:
  0.0 83.0 jit_solution(2221713061619632690)
XLA Ops:
  1.9 74.4 %pool_pair_back.1 = (bf16[2048,1408]{1,0:T(8,128)(2,1)}, bf16[2048,256]{1,0:T(8,128)(2,1)}, f32[128,512]{1,0:T(8,128)}) custom-call(bf16[2048,1408]{1,0:T(8,128)(2,1)} %bitcast.3, bf16[16,1408]{1,0:T(8,128)(2,1)} %bitcast.4, bf16[1408,1408]{1,0:T(8,128)(2,1)} %value_hbm.1, bf16[1408,512]{1,0:T(8,128)(2,1)} %out_hbm.1, bf16[128,512]{1,0:T(8,128)(2,1)} %texts_hbm.3, ...), custom_call_target="tpu_custom_call" | custom-call | tf_op jit(solution)/shard_map/pool_pair_back/pallas_call | solution.py:645
  76.3 6.5 %frame_grads.1 = (bf16[2048,1408]{1,0:T(8,128)(2,1)}, f32[128,512]{1,0:T(8,128)}) custom-call(bf16[2048,1408]{1,0:T(8,128)(2,1)} %get-tuple-element.7.vp_hbm, bf16[2048,256]{1,0:T(8,128)(2,1)} %get-tuple-element.8.sg_hbm, bf16[16,1408]{1,0:T(8,128)(2,1)} %bitcast.5, bf16[128,512]{1,0:T(8,128)(2,1)} %texts_hbm.3, f32[128,512]{1,0:T(8,128)} %get-tuple-element.9.tg_hbm), custom_call_target="tpu_custom_call" | custom-call | tf_op jit(solution)/shard_map/frame_grads/pallas_call | solution.py:661

commit v4 on v3

--- a/solution.py
+++ b/solution.py
@@ -366,7 +366,6 @@
     def sib_rows(rr, carry):
         row = ordered(p1, rr)
         tg_s[0, row] = text_terms(0, row).astype(BF)
-        sib_copy(rr, row).start()
         return carry
 
     lax.fori_loop(0, 4, sib_rows, 0)
@@ -379,23 +378,17 @@
     g3m = remote(vgb_s.at[z3, hhigh], g2_s.at[1, hhigh], zm)
     go(g3p, g3m)
 
-    def own_rows(rr, carry):
-        row = ordered(p2, rr)
-        sib_copy(rr, row).wait_recv()
-        tg_s[1, row] = (text_terms(1, row) + rsib_s[row].astype(F32)).astype(BF)
-        return carry
-
-    tg = tg_s.at[1]
-    lax.fori_loop(0, 1, own_rows, 0)
-    s1p = remote(tg.at[up(p2, 2), low], r1_s.at[0], n2p)
-    s1m = remote(tg.at[up(p2, 2), high], r1_s.at[1], n2m)
-    go(s1p, s1m)
-    lax.fori_loop(1, 2, own_rows, 0)
-    s2p = remote(tg.at[r3, high], r2_s.at[0, high], n2p)
-    go(s2p)
-    lax.fori_loop(2, 3, own_rows, 0)
-    s2m = remote(tg.at[r1, low], r2_s.at[1, low], n2m)
-    go(s2m)
+    def sib_send(rr, carry):
+        sib_copy(rr, ordered(p1, rr)).start()
+        return carry
+
+    lax.fori_loop(0, 4, sib_send, 0)
+
+    def own_rows(row, carry):
+        tg_s[1, row] = text_terms(1, row).astype(BF)
+        return carry
+
+    lax.fori_loop(0, 4, own_rows, 0)
 
     for copy in (g2p, g2m, g3p, g3m):
         copy.wait_recv()
@@ -412,7 +405,22 @@
     eg_m = remote(eg_s, egr_s.at[tm], zm)
     go(eg_p, eg_m)
 
-    lax.fori_loop(3, 4, own_rows, 0)
+    def add_sibling(rr, carry):
+        row = ordered(p2, rr)
+        sib_copy(rr, row).wait_recv()
+        tg_s[1, row] = (tg_s[1, row].astype(F32) + rsib_s[row].astype(F32)).astype(BF)
+        return carry
+
+    tg = tg_s.at[1]
+    lax.fori_loop(0, 1, add_sibling, 0)
+    s1p = remote(tg.at[up(p2, 2), low], r1_s.at[0], n2p)
+    s1m = remote(tg.at[up(p2, 2), high], r1_s.at[1], n2m)
+    go(s1p, s1m)
+    lax.fori_loop(1, 3, add_sibling, 0)
+    s2p = remote(tg.at[r3, high], r2_s.at[0, high], n2p)
+    s2m = remote(tg.at[r1, low], r2_s.at[1, low], n2m)
+    go(s2p, s2m)
+    lax.fori_loop(3, 4, add_sibling, 0)
     eg_p.wait_recv()
     eg_m.wait_recv()
     pg_s[...] = nt(egr_s[...].reshape(clips, emb), ow_s[...]).astype(BF)

time: 83.1 us -> 83 us (level)
  no operation moved by 1% of the time
where the time goes in v4:
time: 83 us; the launch traced here: 82.9 us
  Pallas kernels  80.8 us (97%)
  between operations  2.09 us (3%)
    pallas_call x1, Pallas kernels, local(): pl.pallas_call(functools.partial(main_kernel, (clips, width, head, emb, a...  74.3 us
    pallas_call x1, Pallas kernels, local(): pl.pallas_call(final_kernel, in_specs=[anywhere] * 5, out_specs=(anywhere...  6.5 us

profile of v4, /device:TPU:0, one launch (start us, length us, event | category | flops | bytes accessed | tf_op | source)
XLA Modules:
  0.0 82.9 jit_solution(16445522749754691222)
XLA Ops:
  1.9 74.3 %pool_pair_back.1 = (bf16[2048,1408]{1,0:T(8,128)(2,1)}, bf16[2048,256]{1,0:T(8,128)(2,1)}, f32[128,512]{1,0:T(8,128)}) custom-call(bf16[2048,1408]{1,0:T(8,128)(2,1)} %bitcast.3, bf16[16,1408]{1,0:T(8,128)(2,1)} %bitcast.4, bf16[1408,1408]{1,0:T(8,128)(2,1)} %value_hbm.1, bf16[1408,512]{1,0:T(8,128)(2,1)} %out_hbm.1, bf16[128,512]{1,0:T(8,128)(2,1)} %texts_hbm.3, ...), custom_call_target="tpu_custom_call" | custom-call | tf_op jit(solution)/shard_map/pool_pair_back/pallas_call | solution.py:653
  76.3 6.5 %frame_grads.1 = (bf16[2048,1408]{1,0:T(8,128)(2,1)}, f32[128,512]{1,0:T(8,128)}) custom-call(bf16[2048,1408]{1,0:T(8,128)(2,1)} %get-tuple-element.7.vp_hbm, bf16[2048,256]{1,0:T(8,128)(2,1)} %get-tuple-element.8.sg_hbm, bf16[16,1408]{1,0:T(8,128)(2,1)} %bitcast.5, bf16[128,512]{1,0:T(8,128)(2,1)} %texts_hbm.3, f32[128,512]{1,0:T(8,128)} %get-tuple-element.9.tg_hbm), custom_call_target="tpu_custom_call" | custom-call | tf_op jit(solution)/shard_map/frame_grads/pallas_call | solution.py:669

commit v5 on v4

--- a/solution.py
+++ b/solution.py
@@ -76,11 +76,11 @@
     def up(a, n):
         return lax.rem(a + n, 4)
 
-    p1 = x * (1 - core) + y * core
-    p2 = y * (1 - core) + x * core
+    p1 = y * (1 - core) + x * core
+    p2 = x * (1 - core) + y * core
 
     def plane(a1, a2):
-        return at(a1 * (1 - core) + a2 * core, a2 * (1 - core) + a1 * core, z, core)
+        return at(a2 * (1 - core) + a1 * core, a1 * (1 - core) + a2 * core, z, core)
 
     n1p, n1m = plane(up(p1, 1), p2), plane(up(p1, 3), p2)
     n2p, n2m = plane(p1, up(p2, 1)), plane(p1, up(p2, 3))
@@ -192,7 +192,7 @@
             pq_s[:, clip_part, cols] = pooled.reshape(HEADS, GROUP, pooled.shape[1])
         return carry
 
-    lax.fori_loop(0, groups // 2, pool_group, 0, unroll=4)
+    lax.fori_loop(0, groups // 2, pool_group, 0, unroll=8)
 
     for copy in fwd1:
         copy.wait_recv()
@@ -201,7 +201,7 @@
     go(row_p, row_m)
     sib0 = sib_row(p2)
 
-    lax.fori_loop(groups // 2, groups, pool_group, 0, unroll=4)
+    lax.fori_loop(groups // 2, groups, pool_group, 0, unroll=8)
 
     load_w.wait()
     load_ow.wait()
@@ -302,8 +302,8 @@
 
     def text_base(whose, a2, a1):
         c = core * whose + (1 - core) * (1 - whose)
-        xx = a1 * (1 - c) + a2 * c
-        yy = a2 * (1 - c) + a1 * c
+        xx = a2 * (1 - c) + a1 * c
+        yy = a1 * (1 - c) + a2 * c
         return (tm * 64 + ((z_lo * 4 + xx) * 4 + yy) * 2 + c) * 128
 
     def pair_row(whose, row):
@@ -454,7 +454,7 @@
         u_send[pl.ds(g, 1), :] = jnp.sum(prod * e_s[frame_part, :], axis=0, keepdims=True)
         return carry
 
-    lax.fori_loop(0, groups, score_terms, 0, unroll=4)
+    lax.fori_loop(0, groups, score_terms, 0, unroll=8)
     uc = remote(u_send, u_recv, partner)
     uc.start()
 
@@ -489,7 +489,7 @@
     u2m = remote(tr_s.at[b3, tlow], q2_s.at[1, tlow], n1m)
     go(u1p, u1m, u2p, u2m)
 
-    lax.fori_loop(groups // 4, 3 * groups // 4, value_part, 0, unroll=4)
+    lax.fori_loop(groups // 4, 3 * groups // 4, value_part, 0, unroll=8)
     u1p.wait_recv()
     u1m.wait_recv()
     tr_s[b1, tlow] = (tr_s[b1, tlow].astype(F32) + q1_s[0].astype(F32)).astype(BF)

time: 83 us -> 82.3 us (level)
  no operation moved by 1% of the time
where the time goes in v5:
time: 82.3 us; the launch traced here: 82.2 us
  Pallas kernels  80.1 us (97%)
  between operations  2.11 us (3%)
    pallas_call x1, Pallas kernels, local(): pl.pallas_call(functools.partial(main_kernel, (clips, width, head, emb, a...  73.6 us
    pallas_call x1, Pallas kernels, local(): pl.pallas_call(final_kernel, in_specs=[anywhere] * 5, out_specs=(anywhere...  6.5 us

profile of v5, /device:TPU:0, one launch (start us, length us, event | category | flops | bytes accessed | tf_op | source)
XLA Modules:
  0.0 82.2 jit_solution(17140912926832212319)
XLA Ops:
  1.9 73.6 %pool_pair_back.1 = (bf16[2048,1408]{1,0:T(8,128)(2,1)}, bf16[2048,256]{1,0:T(8,128)(2,1)}, f32[128,512]{1,0:T(8,128)}) custom-call(bf16[2048,1408]{1,0:T(8,128)(2,1)} %bitcast.3, bf16[16,1408]{1,0:T(8,128)(2,1)} %bitcast.4, bf16[1408,1408]{1,0:T(8,128)(2,1)} %value_hbm.1, bf16[1408,512]{1,0:T(8,128)(2,1)} %out_hbm.1, bf16[128,512]{1,0:T(8,128)(2,1)} %texts_hbm.3, ...), custom_call_target="tpu_custom_call" | custom-call | tf_op jit(solution)/shard_map/pool_pair_back/pallas_call | solution.py:653
  75.5 6.5 %frame_grads.1 = (bf16[2048,1408]{1,0:T(8,128)(2,1)}, f32[128,512]{1,0:T(8,128)}) custom-call(bf16[2048,1408]{1,0:T(8,128)(2,1)} %get-tuple-element.7.vp_hbm, bf16[2048,256]{1,0:T(8,128)(2,1)} %get-tuple-element.8.sg_hbm, bf16[16,1408]{1,0:T(8,128)(2,1)} %bitcast.5, bf16[128,512]{1,0:T(8,128)(2,1)} %texts_hbm.3, f32[128,512]{1,0:T(8,128)} %get-tuple-element.9.tg_hbm), custom_call_target="tpu_custom_call" | custom-call | tf_op jit(solution)/shard_map/frame_grads/pallas_call | solution.py:669

commit v6 on v5

--- a/solution.py
+++ b/solution.py
@@ -84,7 +84,8 @@
 
     n1p, n1m = plane(up(p1, 1), p2), plane(up(p1, 3), p2)
     n2p, n2m = plane(p1, up(p2, 1)), plane(p1, up(p2, 3))
-    zp, zm = at(x, y, up(z, 1), core), at(x, y, up(z, 3), core)
+    z1, z2, z3 = up(z, 1 + 2 * core), up(z, 2), up(z, 3 - 2 * core)
+    zp, zm = at(x, y, z1, core), at(x, y, z3, core)
     partner = (1 - tm, ci)
     sibling = at(x, y, z, 1 - core)
 
@@ -237,8 +238,8 @@
     in_head = (head_lane >= head_start) & (head_lane < head_start + head)
     pooled = (acc_s[...] * nn(spread.astype(BF), jnp.where(in_head, 1.0, 0.0).astype(BF))).astype(BF)
     embp_s[...] = nn(pooled, ow_s[...]).astype(BF).reshape(2, half_clips, emb)
-    er_p = remote(embp_s.at[up(z, 1) // 2], embr_s.at[0], zp)
-    er_m = remote(embp_s.at[up(z, 3) // 2], embr_s.at[1], zm)
+    er_p = remote(embp_s.at[z1 // 2], embr_s.at[0], zp)
+    er_m = remote(embp_s.at[z3 // 2], embr_s.at[1], zm)
     go(er_p, er_m)
 
     row_p.wait_recv()
@@ -278,7 +279,6 @@
     v_first = send_vis(z, hlow, zp), send_vis(z, hhigh, zm)
     v_second = send_vis(z, hhigh, zp), send_vis(z, hlow, zm)
     lax.fori_loop(groups // 2, groups, weights, 0, unroll=4)
-    z1, z2, z3 = up(z, 1), up(z, 2), up(z, 3)
     for copy in v_first:
         copy.wait_recv()
     v_far = send_vis(z3, hlow, zp), send_vis(z1, hhigh, zm)
@@ -331,7 +331,7 @@
             pair_row(whose, row)
             return carry
 
-        lax.fori_loop(0, 4, body, 0)
+        lax.fori_loop(0, 4, body, 0, unroll=2)
 
     pair_rows(1)
     for copy in (sib0, sib1, sib2, sib3):
@@ -368,7 +368,7 @@
         tg_s[0, row] = text_terms(0, row).astype(BF)
         return carry
 
-    lax.fori_loop(0, 4, sib_rows, 0)
+    lax.fori_loop(0, 4, sib_rows, 0, unroll=2)
 
     g1p.wait_recv()
     g1m.wait_recv()
@@ -388,7 +388,7 @@
         tg_s[1, row] = text_terms(1, row).astype(BF)
         return carry
 
-    lax.fori_loop(0, 4, own_rows, 0)
+    lax.fori_loop(0, 4, own_rows, 0, unroll=2)
 
     for copy in (g2p, g2m, g3p, g3m):
         copy.wait_recv()

time: 82.3 us -> 81.6 us (level)
  no operation moved by 1% of the time
where the time goes in v6:
time: 81.6 us; the launch traced here: 81.5 us
  Pallas kernels  79.4 us (97%)
  between operations  2.11 us (3%)
    pallas_call x1, Pallas kernels, local(): pl.pallas_call(functools.partial(main_kernel, (clips, width, head, emb, a...  72.9 us
    pallas_call x1, Pallas kernels, local(): pl.pallas_call(final_kernel, in_specs=[anywhere] * 5, out_specs=(anywhere...  6.5 us

profile of v6, /device:TPU:0, one launch (start us, length us, event | category | flops | bytes accessed | tf_op | source)
XLA Modules:
  0.0 81.5 jit_solution(10419350154702770828)
XLA Ops:
  1.9 72.9 %pool_pair_back.1 = (bf16[2048,1408]{1,0:T(8,128)(2,1)}, bf16[2048,256]{1,0:T(8,128)(2,1)}, f32[128,512]{1,0:T(8,128)}) custom-call(bf16[2048,1408]{1,0:T(8,128)(2,1)} %bitcast.3, bf16[16,1408]{1,0:T(8,128)(2,1)} %bitcast.4, bf16[1408,1408]{1,0:T(8,128)(2,1)} %value_hbm.1, bf16[1408,512]{1,0:T(8,128)(2,1)} %out_hbm.1, bf16[128,512]{1,0:T(8,128)(2,1)} %texts_hbm.3, ...), custom_call_target="tpu_custom_call" | custom-call | tf_op jit(solution)/shard_map/pool_pair_back/pallas_call | solution.py:653
  74.8 6.5 %frame_grads.1 = (bf16[2048,1408]{1,0:T(8,128)(2,1)}, f32[128,512]{1,0:T(8,128)}) custom-call(bf16[2048,1408]{1,0:T(8,128)(2,1)} %get-tuple-element.7.vp_hbm, bf16[2048,256]{1,0:T(8,128)(2,1)} %get-tuple-element.8.sg_hbm, bf16[16,1408]{1,0:T(8,128)(2,1)} %bitcast.5, bf16[128,512]{1,0:T(8,128)(2,1)} %texts_hbm.3, f32[128,512]{1,0:T(8,128)} %get-tuple-element.9.tg_hbm), custom_call_target="tpu_custom_call" | custom-call | tf_op jit(solution)/shard_map/frame_grads/pallas_call | solution.py:669

commit v7 on v6

--- a/solution.py
+++ b/solution.py
@@ -143,9 +143,16 @@
     a0m = remote(own.at[p2, p1], own.at[p2, p1], n1m)
     go(a0p, a0m)
 
+    acc_s[...] = jnp.zeros_like(acc_s)
+    vg_s[...] = jnp.zeros_like(vg_s)
+    lanes = HEADS * GROUP
+    head_start = (lax.broadcasted_iota(jnp.int32, (lanes, width), 0) // GROUP) * head
+    head_lane = lax.broadcasted_iota(jnp.int32, (lanes, width), 1)
+    in_head = (head_lane >= head_start) & (head_lane < head_start + head)
+    pg_s[...] = jnp.where(in_head, 1.0, 0.0).astype(BF)
+
     mask = own_clip_mask(frames_here)
     clip_mask = own_clip_mask(1)
-    lanes = HEADS * GROUP
 
     def own_lane(per_clip):
         picked = per_clip.reshape(per_clip.shape[0] // GROUP, GROUP, lanes) * clip_mask[None]
@@ -206,7 +213,6 @@
 
     load_w.wait()
     load_ow.wait()
-    acc_s[...] = jnp.zeros_like(acc_s)
 
     pairs = []
     for h in range(0, HEADS, 2):
@@ -233,10 +239,7 @@
     alpha = mine_f / (ms_send[1] * mine_f + ms_recv[1] * theirs_f)
     alpha_s[...] = alpha
     spread = (alpha[:, None, :] * clip_mask[None]).reshape(clips, lanes)
-    head_start = (lax.broadcasted_iota(jnp.int32, (lanes, width), 0) // GROUP) * head
-    head_lane = lax.broadcasted_iota(jnp.int32, (lanes, width), 1)
-    in_head = (head_lane >= head_start) & (head_lane < head_start + head)
-    pooled = (acc_s[...] * nn(spread.astype(BF), jnp.where(in_head, 1.0, 0.0).astype(BF))).astype(BF)
+    pooled = (acc_s[...] * nn(spread.astype(BF), pg_s[...])).astype(BF)
     embp_s[...] = nn(pooled, ow_s[...]).astype(BF).reshape(2, half_clips, emb)
     er_p = remote(embp_s.at[z1 // 2], embr_s.at[0], zp)
     er_m = remote(embp_s.at[z3 // 2], embr_s.at[1], zm)
@@ -289,7 +292,6 @@
     for copy in v_second + v_far:
         copy.wait_recv()
 
-    vg_s[...] = jnp.zeros_like(vg_s)
     slope = 0.5 * scale_ref[0]
     shift = 0.5 * bias_ref[0]
     diff = lax.broadcasted_iota(jnp.int32, (128, 128), 0) - lax.broadcasted_iota(
@@ -368,7 +370,7 @@
         tg_s[0, row] = text_terms(0, row).astype(BF)
         return carry
 
-    lax.fori_loop(0, 4, sib_rows, 0, unroll=2)
+    lax.fori_loop(0, 4, sib_rows, 0, unroll=4)
 
     g1p.wait_recv()
     g1m.wait_recv()
@@ -388,7 +390,7 @@
         tg_s[1, row] = text_terms(1, row).astype(BF)
         return carry
 
-    lax.fori_loop(0, 4, own_rows, 0, unroll=2)
+    lax.fori_loop(0, 4, own_rows, 0, unroll=4)
 
     for copy in (g2p, g2m, g3p, g3m):
         copy.wait_recv()
@@ -498,7 +500,6 @@
     u3m = remote(tr_s.at[b3, thigh], q2_s.at[1, thigh], n1m)
     go(u3p, u3m)
 
-    lax.fori_loop(3 * groups // 4, groups, value_part, 0, unroll=4)
 
     uc.wait()
     u_send[...] = u_send[...] + u_recv[...]
@@ -511,10 +512,12 @@
 
     sg_out = []
     for i in range(2):
-        lax.fori_loop(i * groups // 2, (i + 1) * groups // 2, score_grads, 0, unroll=4)
+        lax.fori_loop(i * groups // 2, (i + 1) * groups // 2, score_grads, 0, unroll=8)
         part = pl.ds(i * rows // 2, rows // 2)
         sg_out.append(pltpu.make_async_copy(sg_s.at[part], sg_hbm.at[part], load_sem.at[9 + i]))
         sg_out[i].start()
+
+    lax.fori_loop(3 * groups // 4, groups, value_part, 0, unroll=4)
 
     for copy in (u2p, u2m, u3p, u3m):
         copy.wait_recv()

time: 81.6 us -> 82.5 us (1.011)
  Pallas kernels: 79.4 us -> 80.3 us
    pallas_call x1, Pallas kernels: 72.9 us -> 73.8 us  [local(): pl.pallas_call(functools.partial(main_kernel, (clips, width, head, emb, a...]
where the time goes in v7:
time: 82.5 us; the launch traced here: 82.4 us
  Pallas kernels  80.3 us (97%)
  between operations  2.11 us (3%)
    pallas_call x1, Pallas kernels, local(): pl.pallas_call(functools.partial(main_kernel, (clips, width, head, emb, a...  73.8 us
    pallas_call x1, Pallas kernels, local(): pl.pallas_call(final_kernel, in_specs=[anywhere] * 5, out_specs=(anywhere...  6.5 us

profile of v7, /device:TPU:0, one launch (start us, length us, event | category | flops | bytes accessed | tf_op | source)
XLA Modules:
  0.0 82.4 jit_solution(14557620748619619500)
XLA Ops:
  1.9 73.8 %pool_pair_back.1 = (bf16[2048,1408]{1,0:T(8,128)(2,1)}, bf16[2048,256]{1,0:T(8,128)(2,1)}, f32[128,512]{1,0:T(8,128)}) custom-call(bf16[2048,1408]{1,0:T(8,128)(2,1)} %bitcast.3, bf16[16,1408]{1,0:T(8,128)(2,1)} %bitcast.4, bf16[1408,1408]{1,0:T(8,128)(2,1)} %value_hbm.1, bf16[1408,512]{1,0:T(8,128)(2,1)} %out_hbm.1, bf16[128,512]{1,0:T(8,128)(2,1)} %texts_hbm.3, ...), custom_call_target="tpu_custom_call" | custom-call | tf_op jit(solution)/shard_map/pool_pair_back/pallas_call | solution.py:656
  75.7 6.5 %frame_grads.1 = (bf16[2048,1408]{1,0:T(8,128)(2,1)}, f32[128,512]{1,0:T(8,128)}) custom-call(bf16[2048,1408]{1,0:T(8,128)(2,1)} %get-tuple-element.7.vp_hbm, bf16[2048,256]{1,0:T(8,128)(2,1)} %get-tuple-element.8.sg_hbm, bf16[16,1408]{1,0:T(8,128)(2,1)} %bitcast.5, bf16[128,512]{1,0:T(8,128)(2,1)} %texts_hbm.3, f32[128,512]{1,0:T(8,128)} %get-tuple-element.9.tg_hbm), custom_call_target="tpu_custom_call" | custom-call | tf_op jit(solution)/shard_map/frame_grads/pallas_call | solution.py:672

commit v8 on v7

--- a/solution.py
+++ b/solution.py
@@ -333,7 +333,7 @@
             pair_row(whose, row)
             return carry
 
-        lax.fori_loop(0, 4, body, 0, unroll=2)
+        lax.fori_loop(0, 4, body, 0, unroll=4)
 
     pair_rows(1)
     for copy in (sib0, sib1, sib2, sib3):

time: 82.5 us -> 81.4 us (0.987)
  Pallas kernels: 80.3 us -> 79.2 us
    pallas_call x1, Pallas kernels: 73.8 us -> 72.7 us  [local(): pl.pallas_call(functools.partial(main_kernel, (clips, width, head, emb, a...]
where the time goes in v8:
time: 81.4 us; the launch traced here: 81.3 us
  Pallas kernels  79.2 us (97%)
  between operations  2.11 us (3%)
    pallas_call x1, Pallas kernels, local(): pl.pallas_call(functools.partial(main_kernel, (clips, width, head, emb, a...  72.7 us
    pallas_call x1, Pallas kernels, local(): pl.pallas_call(final_kernel, in_specs=[anywhere] * 5, out_specs=(anywhere...  6.5 us

profile of v8, /device:TPU:0, one launch (start us, length us, event | category | flops | bytes accessed | tf_op | source)
XLA Modules:
  0.0 81.3 jit_solution(16621856209764589994)
XLA Ops:
  1.9 72.7 %pool_pair_back.1 = (bf16[2048,1408]{1,0:T(8,128)(2,1)}, bf16[2048,256]{1,0:T(8,128)(2,1)}, f32[128,512]{1,0:T(8,128)}) custom-call(bf16[2048,1408]{1,0:T(8,128)(2,1)} %bitcast.3, bf16[16,1408]{1,0:T(8,128)(2,1)} %bitcast.4, bf16[1408,1408]{1,0:T(8,128)(2,1)} %value_hbm.1, bf16[1408,512]{1,0:T(8,128)(2,1)} %out_hbm.1, bf16[128,512]{1,0:T(8,128)(2,1)} %texts_hbm.3, ...), custom_call_target="tpu_custom_call" | custom-call | tf_op jit(solution)/shard_map/pool_pair_back/pallas_call | solution.py:656
  74.6 6.5 %frame_grads.1 = (bf16[2048,1408]{1,0:T(8,128)(2,1)}, f32[128,512]{1,0:T(8,128)}) custom-call(bf16[2048,1408]{1,0:T(8,128)(2,1)} %get-tuple-element.7.vp_hbm, bf16[2048,256]{1,0:T(8,128)(2,1)} %get-tuple-element.8.sg_hbm, bf16[16,1408]{1,0:T(8,128)(2,1)} %bitcast.5, bf16[128,512]{1,0:T(8,128)(2,1)} %texts_hbm.3, f32[128,512]{1,0:T(8,128)} %get-tuple-element.9.tg_hbm), custom_call_target="tpu_custom_call" | custom-call | tf_op jit(solution)/shard_map/frame_grads/pallas_call | solution.py:672
